TPU v7x, 32 devices: a whole 2x2x4 slice. The times are simulated.
32 devices in a mesh: dp: 8 (over z, x), mp: 4 (over y, core).
Axes of the slice: x: 2, y: 2, z: 4, core: 2. Of those that a mesh axis runs over, the one named last changes fastest.
Arguments:
- tokens: bfloat16 [15360, 512], P('dp'), may hold values from -6 to 6
- cotangent: bfloat16 [15360, 512], P('dp'), may hold values from -6 to 6
- context_sizes: int32 [8, 5], P('dp'), may hold values from 100 to 800, as said below
- query_hoods: int32 [2560], P('dp'), may hold values from 0 to 4
- owners: int32 [64], replicated, may hold values from 0 to 63, as said below
- master_blocks: float32 [64, 512, 128], P('dp', 'mp')
- first_blocks: float32 [64, 512, 128], P('dp', 'mp')
- second_blocks: float32 [64, 512, 128], P('dp', 'mp'), as said below
- left_blocks: float32 [64, 512, 128], P('dp', 'mp'), as said below
- right_blocks: float32 [64, 512, 128], P('dp', 'mp'), as said below
- left_bases: float32 [64, 512, 128], P('dp', 'mp'), may hold values from -1 to 1, as said below
- right_bases: float32 [64, 512, 128], P('dp', 'mp'), may hold values from -1 to 1, as said below
- vector_master: float32 [4096], P(('dp', 'mp'))
- vector_moment: float32 [4096], P(('dp', 'mp')), may hold values from -80 to 80
- vector_square: float32 [4096], P(('dp', 'mp')), may hold values from 399.36 to 6451.2
Outputs:
- layer_out: float32 [15360, 512], P(('dp', 'mp'))
- tokens_grad: float32 [15360, 512], P(('dp', 'mp'))
- first_moment: float32 [64, 512, 128], P('dp', 'mp')
- second_moment: float32 [64, 512, 128], P('dp', 'mp')
- left_stats: float32 [64, 512, 128], P('dp', 'mp')
- right_stats: float32 [64, 512, 128], P('dp', 'mp')
- left_rotation: float32 [64, 512, 128], P('dp', 'mp')
- right_rotation: float32 [64, 512, 128], P('dp', 'mp')
- master_weight: float32 [64, 512, 128], P('dp', 'mp')
- vector_first: float32 [4096], P(('dp', 'mp'))
- vector_second: float32 [4096], P(('dp', 'mp'))
- vector_weight: float32 [4096], P(('dp', 'mp'))
Inputs may be any that keep to these rules, and one draw needn't show every extreme that they name: `context_sizes`: row g holds the 5 context sizes of group g, which sum to 1600; in every row exactly one size is 800 and the smallest is 100 or more. `owners`: a permutation of the 64 slots. `second_blocks`: positive. `left_blocks`: each block is symmetric and positive definite. `right_blocks`: each block is symmetric and positive definite. `left_bases`: each block is orthogonal. `right_bases`: each block is orthogonal.
All inputs are finite; a program needn't handle non-finite values.
Results may differ from a plain program's by a relative error of at most 0.028.
Values may be sent and summed in bfloat16 or wider, within the bound.
A program may use at most 192 MiB of HBM per device.

v0:
```python
from functools import partial

import jax
import jax.numpy as jnp
from jax import lax
from jax.sharding import PartitionSpec as P

D = 512
HD = 128
FF = 1024
LAYERS = 2
BLK = 128
STEP = 10


HIGHEST = lax.Precision.HIGHEST
NORM_EPSILON = 1e-05
ADAM_EPSILON = 1e-08
BETA_ONE = 0.9
BETA_TWO = 0.95
BETA_STATS = 0.95
RATE_MATRIX = 0.12
RATE_VECTOR = 0.6
DECAY_WEIGHT = 0.01
MASK_VALUE = -1e30


def in_blocks(array, dim, length):
    before, after = (array.shape[:dim], array.shape[dim + 1 :])
    return jnp.moveaxis(array.reshape(*before, length, -1, *after), dim, 0)


def summed_on_arrival(array, axis, dim):
    length = lax.axis_size(axis)
    blocks = lax.all_to_all(in_blocks(array, dim, length), axis, 0, 0, tiled=True)
    return jnp.sum(blocks.astype(jnp.float32), axis=0)


def layer_norm(resid, gain, shift):
    center = resid - jnp.mean(resid, axis=-1, keepdims=True)
    scaled = lax.rsqrt(jnp.mean(center * center, axis=-1, keepdims=True) + NORM_EPSILON)
    normed = center * scaled
    return (normed * gain + shift, normed, scaled)


def norm_back(upper, normed, scaled, gain):
    inner = upper * gain
    lower = scaled * (
        inner
        - jnp.mean(inner, axis=-1, keepdims=True)
        - normed * jnp.mean(inner * normed, axis=-1, keepdims=True)
    )
    return (lower, jnp.sum(upper * normed, axis=0), jnp.sum(upper, axis=0))


def inner_rows(left, right):
    return lax.dot_general(
        left, right, (((0,), (0,)), ((), ())), preferred_element_type=jnp.float32
    )


def outer_last(left, right):
    return lax.dot_general(
        left, right, (((1,), (1,)), ((), ())), preferred_element_type=jnp.float32
    )


def tile_shapes(ffs):
    return (
        (D // BLK, 3 * HD // BLK),
        (HD // BLK, D // BLK),
        (D // BLK, ffs // BLK),
        (ffs // BLK, D // BLK),
    )


def unpack_layers(blocks, ffs):
    layers = []
    offset = 0
    for layer_index in range(LAYERS):
        matrices = []
        for row_tiles, column_tiles in tile_shapes(ffs):
            count = row_tiles * column_tiles
            tiles = blocks[offset : offset + count]
            matrices.append(
                tiles.reshape(row_tiles, column_tiles, BLK, BLK)
                .transpose(0, 2, 1, 3)
                .reshape(row_tiles * BLK, column_tiles * BLK)
            )
            offset += count
        layers.append(matrices)
    return layers


def pack_layers(layer_grads, ffs):
    pieces = []
    for matrices in layer_grads:
        for matrix, sizes in zip(matrices, tile_shapes(ffs)):
            row_tiles, column_tiles = sizes
            pieces.append(
                matrix.reshape(row_tiles, BLK, column_tiles, BLK)
                .transpose(0, 2, 1, 3)
                .reshape(row_tiles * column_tiles, BLK, BLK)
            )
    return jnp.concatenate(pieces, axis=0)


def pick_block(rows_here):
    for candidate in range(512, rows_here + 1):
        if rows_here % candidate == 0:
            return candidate
    return rows_here


def branch_total(partial_sum):
    return lax.psum(partial_sum.astype(jnp.bfloat16), "mp").astype(jnp.float32)


def grad_total(partial_sum):
    return lax.psum(partial_sum.astype(jnp.bfloat16), "mp").astype(jnp.float32)


def final_rows(value):
    share = value.shape[0] // lax.axis_size("mp")
    return lax.dynamic_slice_in_dim(value, lax.axis_index("mp") * share, share, 0)


def vector_part(grads):
    arranged = grads.reshape(lax.axis_size("dp"), lax.axis_size("mp"), -1)
    return lax.dynamic_index_in_dim(arranged, lax.axis_index("mp"), 1, keepdims=False).reshape(-1)


def attend(projected, row_hoods, context_rows, block_rows):
    scale = HD ** (-0.5)
    keys = projected[:context_rows, HD : 2 * HD]
    values = projected[:context_rows, 2 * HD :]
    key_hoods = row_hoods[:context_rows]
    count = projected.shape[0] // block_rows

    def one_block(pieces):
        query_block, hood_block = pieces
        scores = jnp.where(
            hood_block[:, None] == key_hoods[None, :],
            outer_last(query_block, keys) * scale,
            MASK_VALUE,
        )
        peak = jnp.max(scores, axis=1, keepdims=True)
        weights = jnp.exp(scores - peak)
        total = jnp.sum(weights, axis=1, keepdims=True)
        output = jnp.dot(
            (weights / total).astype(jnp.bfloat16), values, preferred_element_type=jnp.float32
        )
        return (output.astype(jnp.bfloat16), (peak + jnp.log(total))[:, 0])

    outputs, totals = lax.map(
        one_block,
        (projected[:, :HD].reshape(count, block_rows, HD), row_hoods.reshape(count, block_rows)),
    )
    return (outputs.reshape(-1, HD), totals.reshape(-1))


def attend_back(projected, row_hoods, context_rows, log_totals, heads_grad, block_rows):
    scale = HD ** (-0.5)
    keys = projected[:context_rows, HD : 2 * HD]
    values = projected[:context_rows, 2 * HD :]
    key_hoods = row_hoods[:context_rows]
    count = projected.shape[0] // block_rows

    def one_block(carry, pieces):
        key_grad, value_grad = carry
        query_block, hood_block, total_block, grad_block = pieces
        scores = outer_last(query_block, keys) * scale
        allowed = hood_block[:, None] == key_hoods[None, :]
        probs = jnp.where(allowed, jnp.exp(scores - total_block[:, None]), 0.0)
        value_grad = value_grad + inner_rows(probs.astype(jnp.bfloat16), grad_block)
        prob_grad = outer_last(grad_block, values)
        score_grad = (
            probs * (prob_grad - jnp.sum(probs * prob_grad, axis=1, keepdims=True))
        ).astype(jnp.bfloat16)
        query_grad = jnp.dot(score_grad, keys, preferred_element_type=jnp.float32) * scale
        key_grad = key_grad + inner_rows(score_grad, query_block) * scale
        return ((key_grad, value_grad), query_grad)

    zeros_start = jnp.zeros((context_rows, HD), jnp.float32)
    pieces = (
        projected[:, :HD].reshape(count, block_rows, HD),
        row_hoods.reshape(count, block_rows),
        log_totals.reshape(count, block_rows),
        heads_grad.reshape(count, block_rows, HD),
    )
    carried, query_grad = lax.scan(one_block, (zeros_start, zeros_start), pieces)
    return (query_grad.reshape(-1, HD), jnp.concatenate([carried[0], carried[1]], axis=1))


def forward_layer(stream, low_rows, matrices, gains, row_hoods, context_rows, block_rows):
    joint_weight, out_weight, up_weight, down_weight = matrices
    projected = jnp.dot(low_rows, joint_weight, preferred_element_type=jnp.float32).astype(
        jnp.bfloat16
    )
    heads_out, log_totals = attend(projected, row_hoods, context_rows, block_rows)
    attended = branch_total(jnp.dot(heads_out, out_weight, preferred_element_type=jnp.float32))
    first_norm, first_hat, first_scale = layer_norm(stream + attended, gains[0], gains[1])
    normed_low = first_norm.astype(jnp.bfloat16)
    hidden = jnp.dot(normed_low, up_weight, preferred_element_type=jnp.float32)
    activated = jax.nn.gelu(hidden, approximate=True).astype(jnp.bfloat16)
    mixed = branch_total(jnp.dot(activated, down_weight, preferred_element_type=jnp.float32))
    second_norm, second_hat, second_scale = layer_norm(first_norm + mixed, gains[2], gains[3])
    return (
        second_norm,
        (
            low_rows,
            projected,
            heads_out,
            log_totals,
            first_hat,
            first_scale,
            normed_low,
            hidden,
            activated,
            second_hat,
            second_scale,
        ),
    )


def backward_layer(upper, matrices, gains, kept, row_hoods, context_rows, block_rows):
    joint_weight, out_weight, up_weight, down_weight = matrices
    (
        low_rows,
        projected,
        heads_out,
        log_totals,
        first_hat,
        first_scale,
        normed_low,
        hidden,
        activated,
        second_hat,
        second_scale,
    ) = kept
    second_grad, gain_two, shift_two = norm_back(upper, second_hat, second_scale, gains[2])
    mixed_low = second_grad.astype(jnp.bfloat16)
    down_grad = inner_rows(activated, mixed_low)
    unused_value, gelu_back = jax.vjp(partial(jax.nn.gelu, approximate=True), hidden)
    hidden_grad = gelu_back(outer_last(mixed_low, down_weight))[0].astype(jnp.bfloat16)
    up_grad = inner_rows(normed_low, hidden_grad)
    first_upper = second_grad + grad_total(outer_last(hidden_grad, up_weight))
    first_grad, gain_one, shift_one = norm_back(first_upper, first_hat, first_scale, gains[0])
    attended_low = first_grad.astype(jnp.bfloat16)
    out_grad = inner_rows(heads_out, attended_low)
    heads_grad = outer_last(attended_low, out_weight).astype(jnp.bfloat16)
    query_grad, key_value_grad = attend_back(
        projected, row_hoods, context_rows, log_totals, heads_grad, block_rows
    )
    padding = jnp.zeros((projected.shape[0] - context_rows, 2 * HD), jnp.float32)
    joint_low = jnp.concatenate(
        [query_grad, jnp.concatenate([key_value_grad, padding], axis=0)], axis=1
    ).astype(jnp.bfloat16)
    joint_grad = inner_rows(low_rows, joint_low)
    lower = first_grad + grad_total(outer_last(joint_low, joint_weight))
    return (
        lower,
        (joint_grad, out_grad, up_grad, down_grad),
        jnp.stack([gain_one, shift_one, gain_two, shift_two]),
    )


def orthonormal(matrix):
    gram = jnp.einsum("...ai,...aj->...ij", matrix, matrix, precision=HIGHEST)
    factor = jnp.linalg.cholesky(gram)
    return jnp.swapaxes(
        jax.scipy.linalg.solve_triangular(factor, jnp.swapaxes(matrix, -1, -2), lower=True), -1, -2
    )


def soap_update(grad, first, second, left, right, left_basis, right_basis, master):

    def turn_in(value):
        return jnp.einsum(
            "...ai,...aj,...jk->...ik", left_basis, value, right_basis, precision=HIGHEST
        )

    first_new = BETA_ONE * first + (1.0 - BETA_ONE) * grad
    turned = turn_in(grad)
    second_new = BETA_TWO * second + (1.0 - BETA_TWO) * turned * turned
    direction = (
        turn_in(first_new)
        / (1.0 - BETA_ONE**STEP)
        / (jnp.sqrt(second_new / (1.0 - BETA_TWO**STEP)) + ADAM_EPSILON)
    )
    update = jnp.einsum(
        "...ia,...ab,...jb->...ij", left_basis, direction, right_basis, precision=HIGHEST
    )
    master_new = master - RATE_MATRIX * (update + DECAY_WEIGHT * master)
    left_new = BETA_STATS * left + (1.0 - BETA_STATS) * jnp.einsum(
        "...ik,...jk->...ij", grad, grad, precision=HIGHEST
    )
    right_new = BETA_STATS * right + (1.0 - BETA_STATS) * jnp.einsum(
        "...ki,...kj->...ij", grad, grad, precision=HIGHEST
    )
    left_turn = orthonormal(
        jnp.einsum("...ij,...jk->...ik", left_new, left_basis, precision=HIGHEST)
    )
    right_turn = orthonormal(
        jnp.einsum("...ij,...jk->...ik", right_new, right_basis, precision=HIGHEST)
    )
    return (first_new, second_new, left_new, right_new, left_turn, right_turn, master_new)


def adam_vector(grad, first, second, weight):
    first_new = BETA_ONE * first + (1.0 - BETA_ONE) * grad
    second_new = BETA_TWO * second + (1.0 - BETA_TWO) * grad * grad
    weight_new = weight - RATE_VECTOR * (first_new / (1.0 - BETA_ONE**STEP)) / (
        jnp.sqrt(second_new / (1.0 - BETA_TWO**STEP)) + ADAM_EPSILON
    )
    return (first_new, second_new, weight_new)


def local(
    tokens,
    cotangent,
    context_sizes,
    query_hoods,
    owners,
    master_blocks,
    first_blocks,
    second_blocks,
    left_blocks,
    right_blocks,
    left_bases,
    right_bases,
    vector_master,
    vector_moment,
    vector_square,
):
    ffs = FF // lax.axis_size("mp")
    rows_here = tokens.shape[0]
    context_rows = rows_here - query_hoods.shape[0]
    gathered = lax.all_gather(master_blocks.astype(jnp.bfloat16), "dp", axis=0, tiled=True).astype(
        master_blocks.dtype
    )
    ordered = jnp.take(gathered, owners, axis=0)
    layers = unpack_layers(ordered.astype(jnp.bfloat16), ffs)
    gains = lax.all_gather(vector_master, ("dp", "mp"), axis=0, tiled=True).reshape(LAYERS, 4, D)
    ends = jnp.cumsum(context_sizes[0])
    positions = jnp.arange(context_rows, dtype=jnp.int32)
    context_hoods = jnp.sum((positions[:, None] >= ends[None, :]).astype(jnp.int32), axis=1)
    row_hoods = jnp.concatenate([context_hoods, query_hoods])
    block_rows = pick_block(rows_here)
    stream = tokens.astype(jnp.float32)
    low_rows = tokens
    saved = []
    for layer_index in range(LAYERS):
        stream, kept = forward_layer(
            stream,
            low_rows,
            layers[layer_index],
            gains[layer_index],
            row_hoods,
            context_rows,
            block_rows,
        )
        saved.append(kept)
        if layer_index + 1 < LAYERS:
            low_rows = stream.astype(jnp.bfloat16)
    layer_out = final_rows(stream)
    upper = cotangent.astype(jnp.float32)
    weight_grads = [None] * LAYERS
    norm_grads = [None] * LAYERS
    for layer_index in reversed(range(LAYERS)):
        upper, weight_grads[layer_index], norm_grads[layer_index] = backward_layer(
            upper,
            layers[layer_index],
            gains[layer_index],
            saved[layer_index],
            row_hoods,
            context_rows,
            block_rows,
        )
    tokens_grad = final_rows(upper)
    block_grads = pack_layers(weight_grads, ffs)
    slot_grads = jnp.take(block_grads, jnp.argsort(owners), axis=0)
    vector_terms = vector_part(jnp.stack(norm_grads).reshape(-1))
    reduced, vector_reduced = (
        summed_on_arrival(slot_grads.astype(jnp.bfloat16), "dp", 0),
        summed_on_arrival(vector_terms.astype(jnp.bfloat16), "dp", 0),
    )
    results = soap_update(
        reduced,
        first_blocks,
        second_blocks,
        left_blocks,
        right_blocks,
        left_bases,
        right_bases,
        master_blocks,
    )
    vector_results = adam_vector(vector_reduced, vector_moment, vector_square, vector_master)
    return (layer_out, tokens_grad) + results + vector_results


def solution(mesh):
    return jax.shard_map(
        local,
        mesh=mesh,
        in_specs=(
            P("dp", None),
            P("dp", None),
            P("dp", None),
            P("dp"),
            P(),
            P("dp", "mp", None),
            P("dp", "mp", None),
            P("dp", "mp", None),
            P("dp", "mp", None),
            P("dp", "mp", None),
            P("dp", "mp", None),
            P("dp", "mp", None),
            P(("dp", "mp")),
            P(("dp", "mp")),
            P(("dp", "mp")),
        ),
        out_specs=(
            P(("dp", "mp"), None),
            P(("dp", "mp"), None),
            P("dp", "mp", None),
            P("dp", "mp", None),
            P("dp", "mp", None),
            P("dp", "mp", None),
            P("dp", "mp", None),
            P("dp", "mp", None),
            P("dp", "mp", None),
            P(("dp", "mp")),
            P(("dp", "mp")),
            P(("dp", "mp")),
        ),
        check_vma=False,
    )
```

profile of v0, /device:TPU:0, one launch (start us, length us, event | category | flops | bytes accessed | tf_op | source)
XLA Modules:
  0.0 1059.7 jit_solution(2847916296908636959)
XLA Ops:
  12.2 50.6 %all-gather.3.cloned.1.call-done = bf16[64,128,128]{2,1,0:T(8,128)(2,1)} async-done(((bf16[8,128,128]{2,1,0:T(8,128)(2,1)}), bf16[64,128,128]{2,1,0:T(8,128)(2,1)}) %all-gather.3.cloned.1.call-update) | async-done | bytes 2097168 | tf_op jit(solution)/shard_map/all_gather | solution.py:339
  78.5 11.8 %while.54 = (s32[]{:T(128)}, bf16[3,640,128]{2,1,0:T(8,128)(2,1)}, f32[3,640]{1,0:T(4,128)S(1)}, s32[3,640]{1,0:T(4,128)S(1)}, s32[1600]{0:T(1024)S(1)}, /*index...) while((s32[]{:T(128)}, bf16[3,640,128]{2,1,0:T(8,128)(2,1)}, ...), condition=%wide.region_5.7_spmd, body=%wide.region_2.6_spmd.sunk | while | flops 533585280 | bytes 13479805 | solution.py:155
  93.8 38.8 %all-gather = f32[32,1,128]{2,1,0:T(1,128)S(1)} all-gather(f32[1,1,128]{2,1,0:T(1,128)S(1)} %bitcast.419), channel_id=1, replica_groups=mesh['dp'=8,'mp'=4] {'dp','mp'}, dimensions={0}, use_global_device_ids=true | all-gather | bytes 16896 | tf_op jit(solution)/shard_map/all_gather | solution.py:344
  135.7 6.0 all-reduce.11.cloned.1.call-done
  151.2 48.0 %all-reduce.13.cloned.1.call-done = bf16[1920,512]{1,0:T(8,128)(2,1)} async-done(((bf16[1920,512]{1,0:T(8,128)(2,1)}), bf16[1920,512]{1,0:T(8,128)(2,1)}) %all-reduce.13.cloned.1.call-update) | async-done | bytes 1966096 | tf_op jit(solution)/shard_map/psum | solution.py:116
  206.4 7.3 while.55
  216.3 48.9 %all-reduce.15.cloned.1.call-done = bf16[1920,512]{1,0:T(8,128)(2,1)} async-done(((bf16[1920,512]{1,0:T(8,128)(2,1)}), bf16[1920,512]{1,0:T(8,128)(2,1)}) %all-reduce.15.cloned.1.call-update) | async-done | bytes 1966096 | tf_op jit(solution)/shard_map/psum | solution.py:116
  276.6 10.0 all-reduce.19.cloned.1.call-start
  286.6 39.5 %all-reduce.17.cloned.1.call-done = bf16[1920,512]{1,0:T(8,128)(2,1)} async-done(((bf16[1920,512]{1,0:T(8,128)(2,1)}), bf16[1920,512]{1,0:T(8,128)(2,1)}) %all-reduce.17.cloned.1.call-update) | async-done | bytes 1966096 | tf_op jit(solution)/shard_map/psum | solution.py:116
  345.0 46.3 %all-reduce.19.cloned.1.call-done = bf16[1920,512]{1,0:T(8,128)(2,1)} async-done(((bf16[1920,512]{1,0:T(8,128)(2,1)}), bf16[1920,512]{1,0:T(8,128)(2,1)}) %all-reduce.19.cloned.1.call-update) | async-done | bytes 1966096 | tf_op jit(solution)/shard_map/psum | solution.py:120
  391.3 6.3 multiply_reduce_fusion.2
  405.2 22.9 %while.56 = (s32[]{:T(128)}, f32[1600,128]{1,0:T(8,128)S(1)}, f32[1600,128]{1,0:T(8,128)S(1)}, bf16[3,640,128]{2,1,0:T(8,128)(2,1)}, s32[3,640]{1,0:T(4,128)S(1)...) while((s32[]{:T(128)}, f32[1600,128]{1,0:T(8,128)S(1)}, ...), condition=%wide.region_29.31_spmd.clone, body=%wide.region_27.30_spmd.clone.sunk | while | flops 1322065280 | bytes 43777304 | solution.py:191
  448.0 33.3 %all-reduce.21.cloned.1.call-done = bf16[1920,512]{1,0:T(8,128)(2,1)} async-done(((bf16[1920,512]{1,0:T(8,128)(2,1)}), bf16[1920,512]{1,0:T(8,128)(2,1)}) %all-reduce.21.cloned.1.call-update) | async-done | bytes 1966096 | tf_op jit(solution)/shard_map/psum | solution.py:120
  481.4 6.4 multiply_reduce_fusion.3
  515.2 29.1 %all-reduce.23.cloned.1.call-done = bf16[1920,512]{1,0:T(8,128)(2,1)} async-done(((bf16[1920,512]{1,0:T(8,128)(2,1)}), bf16[1920,512]{1,0:T(8,128)(2,1)}) %all-reduce.23.cloned.1.call-update) | async-done | bytes 1966096 | tf_op jit(solution)/shard_map/psum | solution.py:120
  549.5 5.8 convert_bitcast_fusion
  559.9 5.5 all-to-all-start.1
  569.9 28.6 %while.57 = (s32[]{:T(128)}, f32[1600,128]{1,0:T(8,128)}, f32[1600,128]{1,0:T(8,128)S(1)}, bf16[3,640,128]{2,1,0:T(8,128)(2,1)}, s32[3,640]{1,0:T(4,128)S(1)}, /...) while((s32[]{:T(128)}, f32[1600,128]{1,0:T(8,128)}, ...), condition=%wide.region_38.40_spmd.clone, body=%wide.region_36.39_spmd.clone.sunk | while | flops 1322065280 | bytes 50330960 | solution.py:191
  619.4 6.1 all-to-all-start
  632.5 47.0 %all-reduce.25.cloned.1.call-done = bf16[1920,512]{1,0:T(8,128)(2,1)} async-done(((bf16[1920,512]{1,0:T(8,128)(2,1)}), bf16[1920,512]{1,0:T(8,128)(2,1)}) %all-reduce.25.cloned.1.call-update) | async-done | bytes 1966096 | tf_op jit(solution)/shard_map/psum | solution.py:120
  698.0 94.6 %custom-call.12 = f32[8,128,128]{2,1,0:T(8,128)S(1)} custom-call(f32[8,128,128]{2,1,0:T(8,128)} %fusion.113), custom_call_target="Cholesky" | custom-call | tf_op jit(solution)/shard_map/jit(cholesky)/cholesky | solution.py:270
  793.6 94.6 %custom-call.14 = f32[8,128,128]{2,1,0:T(8,128)S(1)} custom-call(f32[8,128,128]{2,1,0:T(8,128)} %fusion.110), custom_call_target="Cholesky" | custom-call | tf_op jit(solution)/shard_map/jit(cholesky)/cholesky | solution.py:270
  889.6 79.4 %custom-call.15 = f32[8,1,128,128]{2,3,1,0:T(8,128)S(1)} custom-call(f32[8,1,128,128]{3,2,1,0:T(8,128)} %get-tuple-element.679), custom_call_target="InvertDiagBlocksLowerTriangular" | custom-call | tf_op jit(solution)/shard_map/jit(_solve_triangular)/vmap()/triangular_solve | solution.py:272
  971.0 79.6 %custom-call.13 = f32[8,1,128,128]{2,3,1,0:T(8,128)S(1)} custom-call(f32[8,1,128,128]{3,2,1,0:T(8,128)} %get-tuple-element.680), custom_call_target="InvertDiagBlocksLowerTriangular" | custom-call | tf_op jit(solution)/shard_map/jit(_solve_triangular)/vmap()/triangular_solve | solution.py:272
  (514 shorter events, 267.4 us)
Async XLA Ops:
  7.2 680.7 %copy-start = (f32[8,128,128]{2,1,0:T(8,128)S(1)}, f32[8,128,128]{2,1,0:T(8,128)}, u32[]{:S(2)}) copy-start(f32[8,128,128]{2,1,0:T(8,128)} %param.38) | copy-start | bytes 1572868
  7.2 55.6 %all-gather.3.cloned.1.call-start = ((), (), s32[]{:S(2)}) async-start(), calls=%async_computation.2 | async-start | bytes 2359296 | tf_op jit(solution)/shard_map/all_gather | solution.py:339
  9.1 132.6 %all-reduce.11.cloned.1.call-start = ((), (), s32[]{:S(2)}) async-start(), calls=%async_computation.3 | async-start | bytes 3932160 | tf_op jit(solution)/shard_map/psum | solution.py:116
  74.1 16.3 %copy-start.47 = (bf16[1,128,4,128]{1,3,2,0:T(8,128)(2,1)}, bf16[1,128,4,128]{1,3,2,0:T(8,128)(2,1)S(1)}, u32[]{:S(2)}) copy-start(bf16[1,128,4,128]{1,3,2,0:T(8,128)(2,1)S(1)} %copy.292) | copy-start | bytes 393220
  90.4 44.9 %copy-start.16 = (bf16[1600,128]{1,0:T(8,128)(2,1)}, bf16[1600,128]{1,0:T(8,128)(2,1)S(1)}, u32[]{:S(2)}) copy-start(bf16[1600,128]{1,0:T(8,128)(2,1)S(1)} %get-tuple-element.1087) | copy-start | bytes 1228804
  90.4 44.9 %copy-start.18 = (bf16[1600,128]{1,0:T(8,128)(2,1)}, bf16[1600,128]{1,0:T(8,128)(2,1)S(1)}, u32[]{:S(2)}) copy-start(bf16[1600,128]{1,0:T(8,128)(2,1)S(1)} %get-tuple-element.1089) | copy-start | bytes 1228804
  93.7 105.5 %all-reduce.13.cloned.1.call-start = ((), (), s32[]{:S(2)}) async-start(), calls=%async_computation.4 | async-start | bytes 3932160 | tf_op jit(solution)/shard_map/psum | solution.py:116
  133.1 66.1 %copy-start.88 = (f32[4,1,128]{2,1,0:T(1,128)}, f32[4,1,128]{2,1,0:T(1,128)S(1)}, u32[]{:S(2)}) copy-start(f32[4,1,128]{2,1,0:T(1,128)S(1)} %get-tuple-element.688) | copy-start | bytes 6148
  133.1 66.1 %copy-start.91 = (f32[4,1,128]{2,1,0:T(1,128)}, f32[4,1,128]{2,1,0:T(1,128)S(1)}, u32[]{:S(2)}) copy-start(f32[4,1,128]{2,1,0:T(1,128)S(1)} %get-tuple-element.687) | copy-start | bytes 6148
  133.1 200.7 %copy-start.86 = (f32[4,1,128]{2,1,0:T(1,128)}, f32[4,1,128]{2,1,0:T(1,128)S(1)}, u32[]{:S(2)}) copy-start(f32[4,1,128]{2,1,0:T(1,128)S(1)} %get-tuple-element.682) | copy-start | bytes 6148
  144.0 55.2 %copy-start.81 = (f32[1920]{0:T(1024)}, f32[1920]{0:T(1024)S(1)}, u32[]{:S(2)}) copy-start(f32[1920]{0:T(1024)S(1)} %broadcast_multiply_fusion.11) | copy-start | bytes 23044
  145.0 54.2 %copy-start.83 = (f32[1920]{0:T(1024)}, f32[1920]{0:T(1024)S(1)}, u32[]{:S(2)}) copy-start(f32[1920]{0:T(1024)S(1)} %add_rsqrt_fusion.3) | copy-start | bytes 23044
  149.7 115.5 %all-reduce.15.cloned.1.call-start = ((), (), s32[]{:S(2)}) async-start(), calls=%async_computation.5 | async-start | bytes 3932160 | tf_op jit(solution)/shard_map/psum | solution.py:116
  213.7 55.4 %copy-start.17 = (bf16[1600,128]{1,0:T(8,128)(2,1)}, bf16[1600,128]{1,0:T(8,128)(2,1)S(1)}, u32[]{:S(2)}) copy-start(bf16[1600,128]{1,0:T(8,128)(2,1)S(1)} %get-tuple-element.1088) | copy-start | bytes 1228804
  213.7 55.4 %copy-start.20 = (bf16[1600,128]{1,0:T(8,128)(2,1)}, bf16[1600,128]{1,0:T(8,128)(2,1)S(1)}, u32[]{:S(2)}) copy-start(bf16[1600,128]{1,0:T(8,128)(2,1)S(1)} %get-tuple-element.1090) | copy-start | bytes 1228804
  213.7 55.4 %copy-start.23 = (bf16[3,640,128]{2,1,0:T(8,128)(2,1)}, bf16[3,640,128]{2,1,0:T(8,128)(2,1)S(1)}, u32[]{:S(2)}) copy-start(bf16[3,640,128]{2,1,0:T(8,128)(2,1)S(1)} %get-tuple-element.1092) | copy-start | bytes 1474564
  213.7 55.4 %copy-start.34 = (bf16[3,640,128]{2,1,0:T(8,128)(2,1)}, bf16[3,640,128]{2,1,0:T(8,128)(2,1)S(1)}, u32[]{:S(2)}) copy-start(bf16[3,640,128]{2,1,0:T(8,128)(2,1)S(1)} %get-tuple-element.221) | copy-start | bytes 1474564
  215.7 110.3 %all-reduce.17.cloned.1.call-start = ((), (), s32[]{:S(2)}) async-start(), calls=%async_computation.6 | async-start | bytes 3932160 | tf_op jit(solution)/shard_map/psum | solution.py:116
  276.6 114.7 %all-reduce.19.cloned.1.call-start = ((), (), s32[]{:S(2)}) async-start(), calls=%async_computation.7 | async-start | bytes 3932160 | tf_op jit(solution)/shard_map/psum | solution.py:120
  341.8 139.6 %all-reduce.21.cloned.1.call-start = ((), (), s32[]{:S(2)}) async-start(), calls=%async_computation.8 | async-start | bytes 3932160 | tf_op jit(solution)/shard_map/psum | solution.py:120
  431.9 112.4 %all-reduce.23.cloned.1.call-start = ((), (), s32[]{:S(2)}) async-start(), calls=%async_computation.9 | async-start | bytes 3932160 | tf_op jit(solution)/shard_map/psum | solution.py:120
  559.9 59.5 %all-to-all-start.1 = ((bf16[8,1,128]{2,1,0:T(2,128)(2,1)}), bf16[8,1,128]{2,1,0:T(2,128)(2,1)S(1)}, u32[]{:S(2)}, u32[]{:S(2)}) async-start(bf16[8,1,128]{2,1,0:T(2,128)(2,1)} %dynamic-slice_convert_fusion), calls=%async_computation.1 | async-start | bytes 8192 | tf_op jit(solution)/shard_map/all_to_all | solution.py:35
  619.4 62.6 %all-to-all-start = ((bf16[8,8,128,128]{3,2,1,0:T(8,128)(2,1)}), bf16[8,8,128,128]{3,2,1,0:T(8,128)(2,1)S(1)}, u32[]{:S(2)}, u32[]{:S(2)}) async-start(bf16[8,8,128,128]{3,2,1,0:T(8,128)(2,1)} %bitcast.347), calls=%async_computation | async-start | bytes 4194304 | tf_op jit(solution)/shard_map/all_to_all | solution.py:35
  625.6 54.0 %all-reduce.25.cloned.1.call-start = ((), (), s32[]{:S(2)}) async-start(), calls=%async_computation.10 | async-start | bytes 3932160 | tf_op jit(solution)/shard_map/psum | solution.py:120
  (108 other events, 341.7 us)
Sparse Core Ops, SparseCore 0:
  10.7 51.9 all-gather.2
  93.8 47.8 all-reduce.10
  149.9 49.2 all-reduce.12
  215.8 49.3 all-reduce.14
  276.7 49.3 all-reduce.16
  341.9 49.3 all-reduce.18
  432.0 49.3 all-reduce.20
  495.0 49.3 all-reduce.22
  629.7 49.7 all-reduce.24
where the time goes:
time: 1070 us; the launch traced here: 1060 us
  other arithmetic  429 us (40%)
  waiting for transfers between devices  349 us (33%)
  matrix products  128 us (12%)
  local copies, waits for them, and re-layouts  75.9 us (7%)
  blocking collectives  38.8 us (4%)
  starting transfers between devices  22.6 us (2%)
  between operations  15.7 us (1%)
    another operation x6, other arithmetic, orthonormal(): factor = jnp.linalg.cholesky(gram)  189 us
    another operation x4, other arithmetic, orthonormal(): jax.scipy.linalg.solve_triangular(factor, jnp.swapaxes(matrix, -1, -2), l...  160 us
    psum x4, waiting for transfers between devices, grad_total(): return lax.psum(partial_sum.astype(jnp.bfloat16), 'mp').astype(jnp.float32)  156 us
    psum x4, waiting for transfers between devices, branch_total(): return lax.psum(partial_sum.astype(jnp.bfloat16), 'mp').astype(jnp.float32)  142 us
    all_gather x1, waiting for transfers between devices, local(): lax.all_gather(master_blocks.astype(jnp.bfloat16), 'dp', axis=0, tiled=True)  50.6 us
    dot_general x26, matrix products, outer_last(): lax.dot_general(left, right, (((1,), (1,)), ((), ())), preferred_element_...  45.9 us
    dot_general x20, matrix products, inner_rows(): lax.dot_general(left, right, (((0,), (0,)), ((), ())), preferred_element_...  42 us
    all_gather x1, blocking collectives, local(): lax.all_gather(vector_master, ('dp', 'mp'), axis=0, tiled=True)  38.8 us
  transfers between devices with their start and end apart: 11, of which 9 were waited for; matrix products, arithmetic and copies ran while one was open for 10% of the time, Pallas kernels for 0%

commit v1 on v0

--- a/solution.py
+++ b/solution.py
@@ -3,6 +3,8 @@
 import jax
 import jax.numpy as jnp
 from jax import lax
+from jax.experimental import pallas as pl
+from jax.experimental.pallas import tpu as pltpu
 from jax.sharding import PartitionSpec as P
 
 D = 512
@@ -265,46 +267,78 @@
     )
 
 
-def orthonormal(matrix):
-    gram = jnp.einsum("...ai,...aj->...ij", matrix, matrix, precision=HIGHEST)
-    factor = jnp.linalg.cholesky(gram)
-    return jnp.swapaxes(
-        jax.scipy.linalg.solve_triangular(factor, jnp.swapaxes(matrix, -1, -2), lower=True), -1, -2
-    )
-
-
-def soap_update(grad, first, second, left, right, left_basis, right_basis, master):
-
-    def turn_in(value):
-        return jnp.einsum(
-            "...ai,...aj,...jk->...ik", left_basis, value, right_basis, precision=HIGHEST
-        )
-
-    first_new = BETA_ONE * first + (1.0 - BETA_ONE) * grad
-    turned = turn_in(grad)
-    second_new = BETA_TWO * second + (1.0 - BETA_TWO) * turned * turned
-    direction = (
-        turn_in(first_new)
-        / (1.0 - BETA_ONE**STEP)
-        / (jnp.sqrt(second_new / (1.0 - BETA_TWO**STEP)) + ADAM_EPSILON)
-    )
-    update = jnp.einsum(
-        "...ia,...ab,...jb->...ij", left_basis, direction, right_basis, precision=HIGHEST
-    )
-    master_new = master - RATE_MATRIX * (update + DECAY_WEIGHT * master)
-    left_new = BETA_STATS * left + (1.0 - BETA_STATS) * jnp.einsum(
-        "...ik,...jk->...ij", grad, grad, precision=HIGHEST
-    )
-    right_new = BETA_STATS * right + (1.0 - BETA_STATS) * jnp.einsum(
-        "...ki,...kj->...ij", grad, grad, precision=HIGHEST
-    )
-    left_turn = orthonormal(
-        jnp.einsum("...ij,...jk->...ik", left_new, left_basis, precision=HIGHEST)
-    )
-    right_turn = orthonormal(
-        jnp.einsum("...ij,...jk->...ik", right_new, right_basis, precision=HIGHEST)
-    )
-    return (first_new, second_new, left_new, right_new, left_turn, right_turn, master_new)
+def split(x):
+    hi=x.astype(jnp.bfloat16)
+    return hi,(x-hi.astype(jnp.float32)).astype(jnp.bfloat16)
+def dot3(a,b,ca,cb):
+    dims=(((ca,),(cb,)),((),()))
+    ah,al=a; bh,bl=b
+    d=lambda x,y: lax.dot_general(x,y,dims,preferred_element_type=jnp.float32)
+    return d(ah,bh)+(d(ah,bl)+d(al,bh))
+def dotf(a,b,ca,cb):
+    return lax.dot_general(a,b,(((ca,),(cb,)),((),())),preferred_element_type=jnp.float32,precision=lax.Precision.HIGHEST)
+
+def soap_kernel(slots, g_ref,m_ref,v_ref,l_ref,r_ref,ql_ref,qr_ref,w_ref, mo,vo,lo,ro,qlo,qro,wo, x_ref, a_ref):
+    def first(i,_):
+        g=g_ref[i]; ql=split(ql_ref[i]); qr=split(qr_ref[i])
+        gs=split(g)
+        m=BETA_ONE*m_ref[i]+(1-BETA_ONE)*g
+        mo[i]=m
+        def turn(v):
+            return dot3(split(dot3(ql,v,0,0)),qr,1,0)
+        tg=turn(gs)
+        v=BETA_TWO*v_ref[i]+(1-BETA_TWO)*tg*tg
+        vo[i]=v
+        d=turn(split(m))/(1-BETA_ONE**STEP)/(jnp.sqrt(v/(1-BETA_TWO**STEP))+ADAM_EPSILON)
+        u=dot3(split(dot3(ql,split(d),1,0)),qr,1,1)
+        w=w_ref[i]
+        wo[i]=w-RATE_MATRIX*(u+DECAY_WEIGHT*w)
+        ln=BETA_STATS*l_ref[i]+(1-BETA_STATS)*dot3(gs,gs,1,1)
+        rn=BETA_STATS*r_ref[i]+(1-BETA_STATS)*dot3(gs,gs,0,0)
+        lo[i]=ln; ro[i]=rn
+        al=dotf(ln,ql_ref[i],1,0); ar=dotf(rn,qr_ref[i],1,0)
+        a_ref[2*i]=al; a_ref[2*i+1]=ar
+        x_ref[2*i]=dotf(al,al,0,0); x_ref[2*i+1]=dotf(ar,ar,0,0)
+        return 0
+    lax.fori_loop(0,slots,first,0)
+    n=2*slots
+    lane=lax.broadcasted_iota(jnp.int32,(8,BLK),1)
+    sub=lax.broadcasted_iota(jnp.int32,(8,BLK),0)
+    for p in range(BLK//8):
+        def step(kk,_):
+            k=p*8+kk
+            idx=jnp.full((8,BLK),k,jnp.int32)
+            atk=lane==k
+            below=sub>kk
+            rows=[jnp.broadcast_to(x_ref[m,pl.ds(k,1),:],(8,BLK)) for m in range(n)]
+            rinv=[1.0/jnp.take_along_axis(row,idx,axis=1) for row in rows]
+            scaled=[jnp.where(atk,1.0,row)*ri for row,ri in zip(rows,rinv)]
+            for m in range(n):
+                for t in range(p,BLK//8):
+                    v=x_ref[m,t*8:(t+1)*8,:]
+                    f=jnp.take_along_axis(v,idx,axis=1)
+                    new=jnp.where(atk,0.0,v)-f*scaled[m]
+                    if t==p: new=jnp.where(below,new,v)
+                    x_ref[m,t*8:(t+1)*8,:]=new
+            return 0
+        lax.fori_loop(0,8,step,0)
+    r=lax.broadcasted_iota(jnp.int32,(BLK,BLK),0); c=lax.broadcasted_iota(jnp.int32,(BLK,BLK),1)
+    def last(i,_):
+        for s,out in ((0,qlo),(1,qro)):
+            x=x_ref[2*i+s]
+            piv=jnp.sum(jnp.where(r==c,x,0.0),axis=1,keepdims=True)
+            inv=jnp.where(r==c,1.0,jnp.where(r>c,x,0.0))*lax.rsqrt(piv)
+            out[i]=dotf(a_ref[2*i+s],inv,1,1)
+        return 0
+    lax.fori_loop(0,slots,last,0)
+
+def soap(g,m,v,l,r,ql,qr,w):
+    slots=g.shape[0]
+    sh=jax.ShapeDtypeStruct((slots,BLK,BLK),jnp.float32)
+    vm=pl.BlockSpec(memory_space=pltpu.VMEM)
+    return pl.pallas_call(partial(soap_kernel,slots),out_shape=[sh]*7,in_specs=[vm]*8,out_specs=[vm]*7,
+        scratch_shapes=[pltpu.VMEM((2*slots,BLK,BLK),jnp.float32)]*2,
+        compiler_params=pltpu.CompilerParams(vmem_limit_bytes=48<<20),name="soap")(g,m,v,l,r,ql,qr,w)
 
 
 def adam_vector(grad, first, second, weight):
@@ -336,13 +370,15 @@
     ffs = FF // lax.axis_size("mp")
     rows_here = tokens.shape[0]
     context_rows = rows_here - query_hoods.shape[0]
-    gathered = lax.all_gather(master_blocks.astype(jnp.bfloat16), "dp", axis=0, tiled=True).astype(
-        master_blocks.dtype
-    )
-    ordered = jnp.take(gathered, owners, axis=0)
-    layers = unpack_layers(ordered.astype(jnp.bfloat16), ffs)
+    gathered = lax.all_gather(master_blocks.astype(jnp.bfloat16), "dp", axis=0, tiled=True)
+    slots = jnp.arange(owners.shape[0], dtype=jnp.int32)
+    place = (owners[:, None] == slots[None, :]).astype(jnp.bfloat16)
+    ordered = jnp.einsum("bs,sij->bij", place, gathered)
+    layers = unpack_layers(ordered, ffs)
     gains = lax.all_gather(vector_master, ("dp", "mp"), axis=0, tiled=True).reshape(LAYERS, 4, D)
-    ends = jnp.cumsum(context_sizes[0])
+    sizes = context_sizes[0]
+    order = jnp.arange(sizes.shape[0], dtype=jnp.int32)
+    ends = jnp.sum(jnp.where(order[None, :] <= order[:, None], sizes[None, :], 0), axis=1)
     positions = jnp.arange(context_rows, dtype=jnp.int32)
     context_hoods = jnp.sum((positions[:, None] >= ends[None, :]).astype(jnp.int32), axis=1)
     row_hoods = jnp.concatenate([context_hoods, query_hoods])
@@ -379,13 +415,13 @@
         )
     tokens_grad = final_rows(upper)
     block_grads = pack_layers(weight_grads, ffs)
-    slot_grads = jnp.take(block_grads, jnp.argsort(owners), axis=0)
+    slot_grads = jnp.einsum("bs,bij->sij", place, block_grads.astype(jnp.bfloat16))
     vector_terms = vector_part(jnp.stack(norm_grads).reshape(-1))
     reduced, vector_reduced = (
         summed_on_arrival(slot_grads.astype(jnp.bfloat16), "dp", 0),
         summed_on_arrival(vector_terms.astype(jnp.bfloat16), "dp", 0),
     )
-    results = soap_update(
+    results = soap(
         reduced,
         first_blocks,
         second_blocks,

time: 1070 us -> 745 us (0.70)
  other arithmetic: 429 us -> 71.3 us
  Pallas kernels: 0 us -> 46.1 us
  matrix products: 128 us -> 110 us
    another operation x15 -> x4, other arithmetic: 352 us -> 1.37 us  [the longest x6 189 us: orthonormal(): factor = jnp.linalg.cholesky(gram)]
    pallas_call x0 -> x1, Pallas kernels: none -> 46.1 us  [soap(): pl.pallas_call(partial(soap_kernel, slots), out_shape=[sh] * 7, in_specs=...]
    reshape x11 -> x7, local copies, waits for them, and re-layouts: 16 us -> 2.74 us  [pack_layers(): matrix.reshape(row_tiles, BLK, column_tiles, BLK).transpose(0, 2, 1, 3)]
    unnamed x189 -> x181, local copies, waits for them, and re-layouts: 23.9 us -> 14.8 us
  transfers between devices with their start and end apart: 11 -> 11, of which waited for: 9 -> 9; matrix products, arithmetic and copies ran while one was open for 10% -> 12% of each run, Pallas kernels for 0% -> 0%
where the time goes in v1:
time: 745 us; the launch traced here: 736 us
  waiting for transfers between devices  359 us (48%)
  matrix products  110 us (15%)
  other arithmetic  71.3 us (10%)
  local copies, waits for them, and re-layouts  71 us (10%)
  Pallas kernels  46.1 us (6%)
  blocking collectives  38.5 us (5%)
  starting transfers between devices  23.2 us (3%)
  between operations  15.4 us (2%)
    psum x4, waiting for transfers between devices, grad_total(): return lax.psum(partial_sum.astype(jnp.bfloat16), 'mp').astype(jnp.float32)  165 us
    psum x4, waiting for transfers between devices, branch_total(): return lax.psum(partial_sum.astype(jnp.bfloat16), 'mp').astype(jnp.float32)  141 us
    all_gather x1, waiting for transfers between devices, local(): lax.all_gather(master_blocks.astype(jnp.bfloat16), 'dp', axis=0, tiled=True)  52.8 us
    pallas_call x1, Pallas kernels, soap(): pl.pallas_call(partial(soap_kernel, slots), out_shape=[sh] * 7, in_specs=...  46.1 us
    dot_general x20, matrix products, inner_rows(): lax.dot_general(left, right, (((0,), (0,)), ((), ())), preferred_element_...  41.2 us
    dot_general x26, matrix products, outer_last(): lax.dot_general(left, right, (((1,), (1,)), ((), ())), preferred_element_...  40.4 us
    all_gather x1, blocking collectives, local(): lax.all_gather(vector_master, ('dp', 'mp'), axis=0, tiled=True)  38.5 us
    reduce_sum x4, other arithmetic, norm_back(): return (lower, jnp.sum(upper * normed, axis=0), jnp.sum(upper, axis=0))  22.2 us
  transfers between devices with their start and end apart: 11, of which 9 were waited for; matrix products, arithmetic and copies ran while one was open for 12% of the time, Pallas kernels for 0%

profile of v1, /device:TPU:0, one launch (start us, length us, event | category | flops | bytes accessed | tf_op | source)
XLA Modules:
  0.0 735.5 jit_solution(3431944976393760408)
XLA Ops:
  11.6 52.8 %all-gather.3.cloned.1.call-done = bf16[64,128,128]{2,0,1:T(8,128)(2,1)} async-done(((bf16[8,128,128]{2,0,1:T(8,128)(2,1)}), bf16[64,128,128]{2,0,1:T(8,128)(2,1)}) %all-gather.3.cloned.1.call-update) | async-done | bytes 2097168 | tf_op jit(solution)/shard_map/all_gather | solution.py:373
  76.4 15.0 %while.54 = (s32[]{:T(128)}, bf16[3,640,128]{2,1,0:T(8,128)(2,1)}, f32[3,640]{1,0:T(4,128)}, s32[3,640]{1,0:T(4,128)}, s32[1600]{0:T(1024)S(1)}, /*index=5*/bf16...) while((s32[]{:T(128)}, bf16[3,640,128]{2,1,0:T(8,128)(2,1)}, ...), condition=%wide.region_5.6_spmd, body=%wide.region_2.5_spmd.sunk | while | flops 533585280 | bytes 13483133 | solution.py:157
  94.8 38.5 %all-gather = f32[32,1,128]{2,1,0:T(1,128)S(1)} all-gather(f32[1,1,128]{2,1,0:T(1,128)S(1)} %bitcast.377), channel_id=1, replica_groups=mesh['dp'=8,'mp'=4] {'dp','mp'}, dimensions={0}, use_global_device_ids=true | all-gather | bytes 16896 | tf_op jit(solution)/shard_map/all_gather | solution.py:378
  137.6 4.9 all-reduce.11.cloned.1.call-done
  151.3 48.8 %all-reduce.13.cloned.1.call-done = bf16[1920,512]{1,0:T(8,128)(2,1)} async-done(((bf16[1920,512]{1,0:T(8,128)(2,1)}), bf16[1920,512]{1,0:T(8,128)(2,1)}) %all-reduce.13.cloned.1.call-update) | async-done | bytes 1966096 | tf_op jit(solution)/shard_map/psum | solution.py:118
  207.1 9.4 %while.55 = (s32[]{:T(128)}, bf16[3,640,128]{2,1,0:T(8,128)(2,1)S(1)}, f32[3,640]{1,0:T(4,128)S(1)}, s32[3,640]{1,0:T(4,128)}, s32[1600]{0:T(1024)S(1)}, /*index...) while((s32[]{:T(128)}, ...), condition=%wide.region_15.16_spmd, body=%wide.region_12.15_spmd.sunk | while | flops 533585280 | bytes 13486205 | solution.py:157
  218.9 49.1 %all-reduce.15.cloned.1.call-done = bf16[1920,512]{1,0:T(8,128)(2,1)} async-done(((bf16[1920,512]{1,0:T(8,128)(2,1)}), bf16[1920,512]{1,0:T(8,128)(2,1)}) %all-reduce.15.cloned.1.call-update) | async-done | bytes 1966096 | tf_op jit(solution)/shard_map/psum | solution.py:118
  279.4 11.1 %all-reduce.19.cloned.1.call-start = ((), (), s32[]{:S(2)}) async-start(), calls=%async_computation.7 | async-start | bytes 3932160 | tf_op jit(solution)/shard_map/psum | solution.py:122
  290.5 38.4 %all-reduce.17.cloned.1.call-done = bf16[1920,512]{1,0:T(8,128)(2,1)} async-done(((bf16[1920,512]{1,0:T(8,128)(2,1)}), bf16[1920,512]{1,0:T(8,128)(2,1)}) %all-reduce.17.cloned.1.call-update) | async-done | bytes 1966096 | tf_op jit(solution)/shard_map/psum | solution.py:118
  349.4 44.2 %all-reduce.19.cloned.1.call-done = bf16[1920,512]{1,0:T(8,128)(2,1)} async-done(((bf16[1920,512]{1,0:T(8,128)(2,1)}), bf16[1920,512]{1,0:T(8,128)(2,1)}) %all-reduce.19.cloned.1.call-update) | async-done | bytes 1966096 | tf_op jit(solution)/shard_map/psum | solution.py:122
  393.6 6.9 multiply_reduce_fusion.2
  407.7 24.5 %while.56 = (s32[]{:T(128)}, f32[1600,128]{1,0:T(8,128)S(1)}, f32[1600,128]{1,0:T(8,128)S(1)}, bf16[3,640,128]{2,1,0:T(8,128)(2,1)}, s32[3,640]{1,0:T(4,128)}, /...) while((s32[]{:T(128)}, f32[1600,128]{1,0:T(8,128)S(1)}, ...), condition=%wide.region_29.30_spmd.clone, body=%wide.region_27.29_spmd.clone.sunk | while | flops 1322065280 | bytes 43777304 | solution.py:193
  436.0 4.6 convolution_convert_fusion.14
  450.8 34.6 %all-reduce.21.cloned.1.call-done = bf16[1920,512]{1,0:T(8,128)(2,1)} async-done(((bf16[1920,512]{1,0:T(8,128)(2,1)}), bf16[1920,512]{1,0:T(8,128)(2,1)}) %all-reduce.21.cloned.1.call-update) | async-done | bytes 1966096 | tf_op jit(solution)/shard_map/psum | solution.py:122
  485.5 7.2 multiply_reduce_fusion.3
  510.3 38.5 %all-reduce.23.cloned.1.call-done = bf16[1920,512]{1,0:T(8,128)(2,1)} async-done(((bf16[1920,512]{1,0:T(8,128)(2,1)}), bf16[1920,512]{1,0:T(8,128)(2,1)}) %all-reduce.23.cloned.1.call-update) | async-done | bytes 1966096 | tf_op jit(solution)/shard_map/psum | solution.py:122
  548.8 5.2 multiply_reduce_fusion.4
  554.1 5.7 convert_bitcast_fusion
  568.0 5.5 all-to-all-start.1
  577.9 29.4 %while.57 = (s32[]{:T(128)}, f32[1600,128]{1,0:T(8,128)}, f32[1600,128]{1,0:T(8,128)S(1)}, bf16[3,640,128]{2,1,0:T(8,128)(2,1)}, s32[3,640]{1,0:T(4,128)}, /*ind...) while((s32[]{:T(128)}, f32[1600,128]{1,0:T(8,128)}, ...), condition=%wide.region_38.39_spmd.clone, body=%wide.region_36.38_spmd.clone.sunk | while | flops 1322065280 | bytes 50330960 | solution.py:193
  611.4 5.0 concatenate.36
  618.9 6.0 all-to-all-start
  630.7 47.4 %all-reduce.25.cloned.1.call-done = bf16[1920,512]{1,0:T(8,128)(2,1)} async-done(((bf16[1920,512]{1,0:T(8,128)(2,1)}), bf16[1920,512]{1,0:T(8,128)(2,1)}) %all-reduce.25.cloned.1.call-update) | async-done | bytes 1966096 | tf_op jit(solution)/shard_map/psum | solution.py:122
  682.6 46.1 %soap.1 = (f32[8,128,128]{2,1,0:T(8,128)}, f32[8,128,128]{2,1,0:T(8,128)}, f32[8,128,128]{2,1,0:T(8,128)}, f32[8,128,128]{2,1,0:T(8,128)}, f32[8,128,128]{2,1,0:...) custom-call(f32[8,128,128]{2,1,0:T(8,128)S(1)} %copy.243.g_ref, f32[8,128,128]{2,1,0:T(8,128)S(1)} %copy-done.1, ...), custom_call_target="tpu_custom_call" | custom-call | tf_op jit(solution)/shard_map/soap/pallas_call | solution.py:339
  (474 shorter events, 218.8 us)
Async XLA Ops:
  7.2 57.3 %all-gather.3.cloned.1.call-start = ((), (), s32[]{:S(2)}) async-start(), calls=%async_computation.2 | async-start | bytes 2359296 | tf_op jit(solution)/shard_map/all_gather | solution.py:373
  9.3 133.2 %all-reduce.11.cloned.1.call-start = ((), (), s32[]{:S(2)}) async-start(), calls=%async_computation.3 | async-start | bytes 3932160 | tf_op jit(solution)/shard_map/psum | solution.py:118
  11.6 57.9 %copy-start.13 = (bf16[1920,512]{1,0:T(8,128)(2,1)S(1)}, bf16[1920,512]{1,0:T(8,128)(2,1)}, u32[]{:S(2)}) copy-start(bf16[1920,512]{1,0:T(8,128)(2,1)} %param.23) | copy-start | bytes 5898244
  94.8 105.2 %all-reduce.13.cloned.1.call-start = ((), (), s32[]{:S(2)}) async-start(), calls=%async_computation.4 | async-start | bytes 3932160 | tf_op jit(solution)/shard_map/psum | solution.py:118
  133.8 66.2 %copy-start.82 = (f32[4,1,128]{2,1,0:T(1,128)}, f32[4,1,128]{2,1,0:T(1,128)S(1)}, u32[]{:S(2)}) copy-start(f32[4,1,128]{2,1,0:T(1,128)S(1)} %get-tuple-element.578) | copy-start | bytes 6148
  133.8 66.2 %copy-start.91 = (f32[4,1,128]{2,1,0:T(1,128)}, f32[4,1,128]{2,1,0:T(1,128)S(1)}, u32[]{:S(2)}) copy-start(f32[4,1,128]{2,1,0:T(1,128)S(1)} %get-tuple-element.577) | copy-start | bytes 6148
  133.8 134.2 %copy-start.78 = (f32[4,1,128]{2,1,0:T(1,128)}, f32[4,1,128]{2,1,0:T(1,128)S(1)}, u32[]{:S(2)}) copy-start(f32[4,1,128]{2,1,0:T(1,128)S(1)} %get-tuple-element.576) | copy-start | bytes 6148
  133.8 203.4 %copy-start.80 = (f32[4,1,128]{2,1,0:T(1,128)}, f32[4,1,128]{2,1,0:T(1,128)S(1)}, u32[]{:S(2)}) copy-start(f32[4,1,128]{2,1,0:T(1,128)S(1)} %get-tuple-element.572) | copy-start | bytes 6148
  144.8 55.2 %copy-start.72 = (f32[1920]{0:T(1024)}, f32[1920]{0:T(1024)S(1)}, u32[]{:S(2)}) copy-start(f32[1920]{0:T(1024)S(1)} %broadcast_multiply_fusion.11) | copy-start | bytes 23044
  150.6 117.5 %all-reduce.15.cloned.1.call-start = ((), (), s32[]{:S(2)}) async-start(), calls=%async_computation.5 | async-start | bytes 3932160 | tf_op jit(solution)/shard_map/psum | solution.py:118
  204.5 63.6 %copy-start.74 = (f32[1920]{0:T(1024)}, f32[1920]{0:T(1024)S(1)}, u32[]{:S(2)}) copy-start(f32[1920]{0:T(1024)S(1)} %add_rsqrt_fusion.2) | copy-start | bytes 23044
  216.5 55.3 %copy-start.26 = (bf16[1600,128]{1,0:T(8,128)(2,1)}, bf16[1600,128]{1,0:T(8,128)(2,1)S(1)}, u32[]{:S(2)}) copy-start(bf16[1600,128]{1,0:T(8,128)(2,1)S(1)} %get-tuple-element.980) | copy-start | bytes 1228804
  216.5 55.3 %copy-start.31 = (bf16[3,640,128]{2,1,0:T(8,128)(2,1)}, bf16[3,640,128]{2,1,0:T(8,128)(2,1)S(1)}, u32[]{:S(2)}) copy-start(bf16[3,640,128]{2,1,0:T(8,128)(2,1)S(1)} %get-tuple-element.982) | copy-start | bytes 1474564
  216.6 55.3 %copy-start.38 = (bf16[3,640,128]{2,1,0:T(8,128)(2,1)}, bf16[3,640,128]{2,1,0:T(8,128)(2,1)S(1)}, u32[]{:S(2)}) copy-start(bf16[3,640,128]{2,1,0:T(8,128)(2,1)S(1)} %get-tuple-element.224) | copy-start | bytes 1474564
  218.5 110.4 %all-reduce.17.cloned.1.call-start = ((), (), s32[]{:S(2)}) async-start(), calls=%async_computation.6 | async-start | bytes 3932160 | tf_op jit(solution)/shard_map/psum | solution.py:118
  218.9 57.1 %copy-start.70 = (bf16[2,4,128,128]{3,1,2,0:T(4,128)(2,1)}, bf16[2,4,128,128]{3,1,2,0:T(4,128)(2,1)S(1)}, u32[]{:S(2)}) copy-start(bf16[2,4,128,128]{3,1,2,0:T(4,128)(2,1)S(1)} %copy.223) | copy-start | bytes 786436
  279.4 114.2 %all-reduce.19.cloned.1.call-start = ((), (), s32[]{:S(2)}) async-start(), calls=%async_computation.7 | async-start | bytes 3932160 | tf_op jit(solution)/shard_map/psum | solution.py:122
  344.2 141.3 %all-reduce.21.cloned.1.call-start = ((), (), s32[]{:S(2)}) async-start(), calls=%async_computation.8 | async-start | bytes 3932160 | tf_op jit(solution)/shard_map/psum | solution.py:122
  436.0 112.9 %all-reduce.23.cloned.1.call-start = ((), (), s32[]{:S(2)}) async-start(), calls=%async_computation.9 | async-start | bytes 3932160 | tf_op jit(solution)/shard_map/psum | solution.py:122
  568.0 51.0 %all-to-all-start.1 = ((bf16[8,1,128]{2,1,0:T(2,128)(2,1)}), bf16[8,1,128]{2,1,0:T(2,128)(2,1)S(1)}, u32[]{:S(2)}, u32[]{:S(2)}) async-start(bf16[8,1,128]{2,1,0:T(2,128)(2,1)} %dynamic-slice_convert_fusion), calls=%async_computation.1 | async-start | bytes 8192 | tf_op jit(solution)/shard_map/all_to_all | solution.py:37
  618.9 61.5 %all-to-all-start = ((bf16[8,8,128,128]{3,1,2,0:T(8,128)(2,1)}), bf16[8,8,128,128]{3,1,2,0:T(8,128)(2,1)}, u32[]{:S(2)}, u32[]{:S(2)}) async-start(bf16[8,8,128,128]{3,1,2,0:T(8,128)(2,1)} %copy.241), calls=%async_computation | async-start | bytes 4194304 | tf_op jit(solution)/shard_map/all_to_all | solution.py:37
  625.0 53.1 %all-reduce.25.cloned.1.call-start = ((), (), s32[]{:S(2)}) async-start(), calls=%async_computation.10 | async-start | bytes 3932160 | tf_op jit(solution)/shard_map/psum | solution.py:122
  627.6 55.0 %copy-start = (f32[8,128,128]{2,1,0:T(8,128)S(1)}, f32[8,128,128]{2,1,0:T(8,128)}, u32[]{:S(2)}) copy-start(f32[8,128,128]{2,1,0:T(8,128)} %w_ref.1) | copy-start | bytes 1572868
  627.6 55.0 %copy-start.1 = (f32[8,128,128]{2,1,0:T(8,128)S(1)}, f32[8,128,128]{2,1,0:T(8,128)}, u32[]{:S(2)}) copy-start(f32[8,128,128]{2,1,0:T(8,128)} %m_ref.1) | copy-start | bytes 1572868
  (107 other events, 971.9 us)
Sparse Core Ops, SparseCore 0:
  10.6 53.7 all-gather.2
  94.9 47.5 all-reduce.10
  150.7 49.2 all-reduce.12
  218.7 49.3 all-reduce.14
  279.5 49.3 all-reduce.16
  344.3 49.3 all-reduce.18
  436.1 49.3 all-reduce.20
  499.5 49.3 all-reduce.22
  628.2 49.7 all-reduce.24

commit v2 on v1

v2 whole, which is shorter than its diff:
```python
import math
from functools import partial

import jax
import jax.numpy as jnp
from jax import lax
from jax.experimental import pallas as pl
from jax.experimental.pallas import tpu as pltpu
from jax.sharding import PartitionSpec as P

RATE_VECTOR = 0.6
MESH=pl.DeviceIdType.MESH
VMEM_SPEC=pl.BlockSpec(memory_space=pltpu.VMEM)
ANY_SPEC=pl.BlockSpec(memory_space=pl.ANY)

def remote(src,dst,send,recv,device):
    return pltpu.make_async_remote_copy(src_ref=src,dst_ref=dst,send_sem=send,recv_sem=recv,device_id=device,device_id_type=MESH)

class Spot:
    def __init__(self,planes):
        dp,mp=lax.axis_index("dp"),lax.axis_index("mp")
        self.dp,self.mp,self.planes=dp,mp,planes
        self.z,self.x=dp//2,dp%2
        self.y,self.c=mp//2,mp%2
        self.across_x=(dp+1-2*self.x,mp)
        self.across_y=(dp,(mp+2)%4)
        self.sibling=(dp,mp+1-2*self.c)
        self.up=(jnp.minimum(dp+2,2*planes-1),mp)
        self.down=(jnp.maximum(dp-2,0),mp)
    def greet(self):
        bar=pltpu.get_barrier_semaphore()
        for who in (self.across_x,self.across_y,self.sibling):
            pl.semaphore_signal(bar,inc=1,device_id=who,device_id_type=MESH)
        @pl.when(self.z<self.planes-1)
        def _(): pl.semaphore_signal(bar,inc=1,device_id=self.up,device_id_type=MESH)
        @pl.when(self.z>0)
        def _(): pl.semaphore_signal(bar,inc=1,device_id=self.down,device_id_type=MESH)
        pl.semaphore_wait(bar,3+jnp.minimum(self.z,1)+jnp.minimum(self.planes-1-self.z,1))
    def ring(self,r,action):
        if r==0:
            action(self.z,None); return
        @pl.when(self.z>=r)
        def _(): action(self.z-r,True)
        @pl.when(self.z+r<self.planes)
        def _(): action(self.z+r,False)

def gather_kernel(planes,half,slab,out,send,recv,zsend,zrecv,lsem):
    s=Spot(planes); rows=slab.shape[0]; z,x,y,c,mp=s.z,s.x,s.y,s.c,s.mp
    A,B=pl.ds(0,half),pl.ds(half,rows-half)
    mx,my=s.across_x,s.across_y
    own=pltpu.make_async_copy(slab,out.at[s.dp,mp],lsem); own.start()
    s.greet()
    def at(p,xx,yy,cc): return out.at[p*2+xx,yy*2+cc]
    xo,yo=1-x,1-y
    def copies(p,src):
        here=at(p,x,y,c) if src is None else src
        f=lambda k,a,b,w: remote(a,b,send.at[k,p],recv.at[k,p],w)
        return dict(
            xown=lambda: f(0,here,at(p,x,y,c),mx), yown=lambda: f(1,here,at(p,x,y,c),my), cown=lambda: f(2,here,at(p,x,y,c),s.sibling),
            yfwd=lambda: f(3,at(p,xo,y,c).at[A],at(p,xo,y,c).at[A],my),
            xfwd=lambda: f(4,at(p,x,yo,c).at[B],at(p,x,yo,c).at[B],mx),
            cx=lambda: f(5,at(p,xo,y,c),at(p,xo,y,c),s.sibling), cy=lambda: f(6,at(p,x,yo,c),at(p,x,yo,c),s.sibling),
            ca=lambda: f(7,at(p,xo,yo,c).at[A],at(p,xo,yo,c).at[A],s.sibling),
            cb=lambda: f(8,at(p,xo,yo,c).at[B],at(p,xo,yo,c).at[B],s.sibling))
    def zcopy(p,up,src=None):
        here=at(p,x,y,c) if src is None else src
        return remote(here,at(p,x,y,c),zsend.at[0 if up else 1,p],zrecv.at[p],s.up if up else s.down)
    def arrive(r):
        def act(p,below):
            src=None
            if below is None: src=slab
            else: zcopy(p,below).wait_recv()
            if below is None or below:
                @pl.when(z<planes-1)
                def _(): zcopy(p,True,src).start()
            if below is None or not below:
                @pl.when(z>0)
                def _(): zcopy(p,False,src).start()
            k=copies(p,src)
            k["xown"]().start(); k["yown"]().start(); k["cown"]().start()
        s.ring(r,act)
    def second(r):
        def act(p,below):
            k=copies(p,None)
            k["xown"]().wait_recv(); k["yfwd"]().start(); k["cx"]().start()
            k["yown"]().wait_recv(); k["xfwd"]().start(); k["cy"]().start()
        s.ring(r,act)
    def third(r):
        def act(p,below):
            k=copies(p,None)
            k["yfwd"]().wait_recv(); k["ca"]().start()
            k["xfwd"]().wait_recv(); k["cb"]().start()
        s.ring(r,act)
    def finish(r):
        def act(p,below):
            src=slab if below is None else None
            k=copies(p,src)
            for n in ("cown","cx","cy","ca","cb"): k[n]().wait_recv()
            for n in k: k[n]().wait_send()
            if below is None or below:
                @pl.when(z<planes-1)
                def _(): zcopy(p,True,src).wait_send()
            if below is None or not below:
                @pl.when(z>0)
                def _(): zcopy(p,False,src).wait_send()
        s.ring(r,act)
    for r in range(planes+2):
        if r<planes: arrive(r)
        if 1<=r<=planes: second(r-1)
        if r>=2: third(r-2)
    for r in range(planes): finish(r)
    own.wait()

def gather_all(slab,dp,collective):
    rows=slab.shape[0]; planes=dp//2; half=rows//2//16*16
    dma=pltpu.SemaphoreType.DMA
    return pl.pallas_call(partial(gather_kernel,planes,half),
        out_shape=jax.ShapeDtypeStruct((dp,4,rows,slab.shape[1]),slab.dtype),
        in_specs=[ANY_SPEC],out_specs=ANY_SPEC,
        scratch_shapes=[dma((9,planes)),dma((9,planes)),dma((2,planes)),dma((planes,)),dma],
        compiler_params=pltpu.CompilerParams(collective_id=collective,has_side_effects=True),name="gather_all")(slab)

def reduce_kernel(planes,half,g,out,rc,acc,ya,xb,xa,yb,own,zin,send,recv,zsend,zrecv):
    s=Spot(planes); rows=g.shape[2]; z,x,y,c,mp=s.z,s.x,s.y,s.c,s.mp
    A,B=pl.ds(0,half),pl.ds(half,rows-half)
    mx,my=s.across_x,s.across_y
    xo,yo,co=1-x,1-y,1-c
    s.greet()
    f32=lambda v: v.astype(jnp.float32)
    def core(p,xx,yy):
        k=xx*2+yy
        return remote(g.at[p*2+xx,yy*2+co],rc.at[p*4+k],send.at[k,p],recv.at[k,p],s.sibling)
    def toya(p,xx): return remote(acc.at[p*4+xx*2+yo,A],ya.at[p*2+xx],send.at[4+xx,p],recv.at[4+xx,p],my)
    def toxb(p,yy): return remote(acc.at[p*4+xo*2+yy,B],xb.at[p*2+yy],send.at[6+yy,p],recv.at[6+yy,p],mx)
    def toxa(p): return remote(ya.at[p*2+xo],xa.at[p],send.at[8,p],recv.at[8,p],mx)
    def toyb(p): return remote(xb.at[p*2+yo],yb.at[p],send.at[9,p],recv.at[9,p],my)
    def toz(p,up): return remote(own.at[p],zin.at[0 if up else 1,p],zsend.at[p],zrecv.at[0 if up else 1,p],s.up if up else s.down)
    def start(p,_):
        for xx in (0,1):
            for yy in (0,1): core(p,xx,yy).start()
    def first(p,_):
        for xx in (0,1):
            for yy in (0,1):
                core(p,xx,yy).wait_recv()
                acc[p*4+xx*2+yy]=(f32(g[p*2+xx,yy*2+c])+f32(rc[p*4+xx*2+yy])).astype(acc.dtype)
        for e in (0,1): toya(p,e).start(); toxb(p,e).start()
    def second(p,_):
        for e in (0,1):
            toya(p,e).wait_recv()
            ya[p*2+e]=(f32(acc[p*4+e*2+y,A])+f32(ya[p*2+e])).astype(ya.dtype)
        toxa(p).start()
        for e in (0,1):
            toxb(p,e).wait_recv()
            xb[p*2+e]=(f32(acc[p*4+x*2+e,B])+f32(xb[p*2+e])).astype(xb.dtype)
        toyb(p).start()
    def third(p,below):
        toxa(p).wait_recv()
        av=f32(ya[p*2+x])+f32(xa[p])
        toyb(p).wait_recv()
        bv=f32(xb[p*2+y])+f32(yb[p])
        if below is None:
            out[A]=av; out[B]=bv
            @pl.when(z>0)
            def _():
                toz(p,True).wait_recv()
                out[...]=out[...]+f32(zin[0,p])
            @pl.when(z<planes-1)
            def _():
                toz(p,False).wait_recv()
                out[...]=out[...]+f32(zin[1,p])
            return
        own[p,A]=av.astype(own.dtype); own[p,B]=bv.astype(own.dtype)
        up=not below
        has=(z>0) if up else (z<planes-1)
        @pl.when(has)
        def _():
            toz(p,up).wait_recv()
            own[p,A]=(av+f32(zin[0 if up else 1,p,A])).astype(own.dtype)
            own[p,B]=(bv+f32(zin[0 if up else 1,p,B])).astype(own.dtype)
        toz(p,up).start()
    def finish(p,below):
        for xx in (0,1):
            for yy in (0,1): core(p,xx,yy).wait_send()
        for e in (0,1): toya(p,e).wait_send(); toxb(p,e).wait_send()
        toxa(p).wait_send(); toyb(p).wait_send()
        if below is not None: toz(p,not below).wait_send()
    order=list(range(planes-1,-1,-1))
    for r in order: s.ring(r,start)
    n=len(order)
    for i in range(n+2):
        if i<n: s.ring(order[i],first)
        if 0<=i-1<n: s.ring(order[i-1],second)
        if 0<=i-2<n: s.ring(order[i-2],third)
    for r in order: s.ring(r,finish)

def reduce_all(g,collective):
    dp,_,rows,cols=g.shape; planes=dp//2; half=rows//2//16*16
    dma=pltpu.SemaphoreType.DMA; bf=lambda *sh: pltpu.VMEM(sh+(cols,),g.dtype)
    return pl.pallas_call(partial(reduce_kernel,planes,half),
        out_shape=jax.ShapeDtypeStruct((rows,cols),jnp.float32),in_specs=[VMEM_SPEC],out_specs=VMEM_SPEC,
        scratch_shapes=[bf(planes*4,rows),bf(planes*4,rows),bf(planes*2,half),bf(planes*2,rows-half),bf(planes,half),bf(planes,rows-half),
            bf(planes,rows),bf(2,planes,rows),dma((10,planes)),dma((10,planes)),dma((planes,)),dma((2,planes))],
        compiler_params=pltpu.CompilerParams(collective_id=collective,has_side_effects=True,vmem_limit_bytes=56<<20),name="reduce_all")(g)

def share_kernel(mine,full,send,recv,lsem):
    s=Spot(1); rows=mine.shape[0]; n=send.shape[1]; step=rows//n
    bar=pltpu.get_barrier_semaphore()
    for who in (s.across_y,s.sibling): pl.semaphore_signal(bar,inc=1,device_id=who,device_id_type=MESH)
    local=pltpu.make_async_copy(mine,full.at[s.mp],lsem); local.start()
    pl.semaphore_wait(bar,2)
    far=s.across_y[1]
    part=lambda i: pl.ds(i*step,step)
    over=lambda i: remote(mine.at[part(i)],full.at[s.mp,part(i)],send.at[0,i],recv.at[0,i],s.across_y)
    near=lambda i: remote(mine.at[part(i)],full.at[s.mp,part(i)],send.at[1,i],recv.at[1,i],s.sibling)
    on=lambda i: remote(full.at[far,part(i)],full.at[far,part(i)],send.at[2,i],recv.at[2,i],s.sibling)
    for i in range(n): over(i).start()
    for i in range(n): near(i).start()
    for i in range(n):
        over(i).wait_recv(); on(i).start()
    for i in range(n):
        near(i).wait_recv(); on(i).wait_recv()
        for k in (over,near,on): k(i).wait_send()
    local.wait()

def share_rows(mine,collective,n=3):
    rows,cols=mine.shape; dma=pltpu.SemaphoreType.DMA
    out=pl.pallas_call(share_kernel,out_shape=jax.ShapeDtypeStruct((4,rows,cols),mine.dtype),in_specs=[VMEM_SPEC],out_specs=VMEM_SPEC,
        scratch_shapes=[dma((3,n)),dma((3,n)),dma],
        compiler_params=pltpu.CompilerParams(collective_id=collective,has_side_effects=True,vmem_limit_bytes=24<<20),name="share_rows")(mine)
    return out.reshape(4*rows,cols)

def total_kernel(terms,own,out,rc,acc,ry,send,recv):
    s=Spot(1); rows=own.shape[0]; n=send.shape[1]; step=rows//n
    bar=pltpu.get_barrier_semaphore()
    for who in (s.across_y,s.sibling): pl.semaphore_signal(bar,inc=1,device_id=who,device_id_type=MESH)
    pl.semaphore_wait(bar,2)
    far=s.across_y[1]; co=1-s.c
    part=lambda i: pl.ds(i*step,step)
    f32=lambda v: v.astype(jnp.float32)
    a=lambda i: remote(terms.at[(1-s.y)*2+co,part(i)],rc.at[0,part(i)],send.at[0,i],recv.at[0,i],s.sibling)
    b=lambda i: remote(terms.at[s.y*2+co,part(i)],rc.at[1,part(i)],send.at[1,i],recv.at[1,i],s.sibling)
    o=lambda i: remote(acc.at[part(i)],ry.at[part(i)],send.at[2,i],recv.at[2,i],s.across_y)
    for i in range(n): a(i).start()
    for i in range(n): b(i).start()
    for i in range(n):
        a(i).wait_recv()
        acc[part(i)]=(f32(terms[far,part(i)])+f32(rc[0,part(i)])).astype(acc.dtype)
        o(i).start()
    for i in range(n):
        b(i).wait_recv()
        out[part(i)]=own[part(i)]+(f32(terms[s.mp,part(i)])+f32(rc[1,part(i)]))
    for i in range(n):
        o(i).wait_recv()
        out[part(i)]=out[part(i)]+f32(ry[part(i)])
    for i in range(n):
        for k in (a,b,o): k(i).wait_send()

def total_rows(terms,own,collective,n=3):
    rows,cols=own.shape; dma=pltpu.SemaphoreType.DMA
    return pl.pallas_call(total_kernel,out_shape=jax.ShapeDtypeStruct((rows,cols),jnp.float32),in_specs=[VMEM_SPEC]*2,out_specs=VMEM_SPEC,
        scratch_shapes=[pltpu.VMEM((2,rows,cols),terms.dtype),pltpu.VMEM((rows,cols),terms.dtype),pltpu.VMEM((rows,cols),terms.dtype),dma((3,n)),dma((3,n))],
        compiler_params=pltpu.CompilerParams(collective_id=collective,has_side_effects=True,vmem_limit_bytes=24<<20),name="total_rows")(terms.reshape(4,rows,cols),own)
D=512; HD=128; FF=1024; LAYERS=2; BLK=128
NORM_EPSILON=1e-5; MASK_VALUE=-1e30
HEADS=4
f32=jnp.float32; bf16=jnp.bfloat16
VMEM_SPEC=pl.BlockSpec(memory_space=pltpu.VMEM)
ANY_SPEC=pl.BlockSpec(memory_space=pl.ANY)
SMEM_SPEC=pl.BlockSpec(memory_space=pltpu.SMEM)
SCALE=HD**-0.5; LOG2E=math.log2(math.e)
ROOT=math.sqrt(2/math.pi)

def nn(a,b): return lax.dot_general(a,b,(((1,),(0,)),((),())),preferred_element_type=f32)
def nt(a,b): return lax.dot_general(a,b,(((1,),(1,)),((),())),preferred_element_type=f32)
def tn(a,b): return lax.dot_general(a,b,(((0,),(0,)),((),())),preferred_element_type=f32)

def normed(r):
    center=r-jnp.mean(r,axis=-1,keepdims=True)
    rho=lax.rsqrt(jnp.mean(center*center,axis=-1,keepdims=True)+NORM_EPSILON)
    return center*rho,rho
def norm_back(dy,xhat,rho,gain):
    inner=dy*gain
    return rho*(inner-jnp.mean(inner,axis=-1,keepdims=True)-xhat*jnp.mean(inner*xhat,axis=-1,keepdims=True))
def gelu(v): return 0.5*v*(1+jnp.tanh(ROOT*(v+0.044715*v*v*v)))
def gelu_both(v):
    sq=v*v
    t=jnp.tanh(ROOT*v*(1+0.044715*sq))
    half=0.5*(1+t)
    return v*half,half+0.5*v*(1-t*t)*(ROOT*(1+3*0.044715*sq))

ROWS_TILE=(4,1,4,2); COLS_TILE=(3,4,2,4)
FIRST_BLOCK=(0,12,16,24)
LAYER_BLOCKS=32

def weight_shapes():
    return [pltpu.VMEM((D,D),bf16),pltpu.VMEM((HEADS,D,2*HD),bf16),pltpu.VMEM((D,D),bf16),pltpu.VMEM((D,FF),bf16),pltpu.VMEM((FF,D),bf16)]

class Weights:
    def __init__(self,layer,owners,wall,slots,refs,sems):
        self.q,self.kv,self.out,self.up,self.down=refs
        self.sems=sems
        fs=FF//HEADS
        def tile(kind,r,c,j,dst,sem):
            slot=owners[layer*LAYER_BLOCKS+FIRST_BLOCK[kind]+r*COLS_TILE[kind]+c]
            src=wall.at[slot//slots,j,pl.ds(pl.multiple_of(slot%slots*BLK,BLK),BLK),:]
            pltpu.make_async_copy(src,dst,sems.at[sem]).start()
        for r in range(4):
            for c in (1,2):
                for j in range(HEADS): tile(0,r,c,j,self.kv.at[j,r*BLK:(r+1)*BLK,(c-1)*BLK:c*BLK],1)
        for r in range(4):
            for j in range(HEADS): tile(0,r,0,j,self.q.at[r*BLK:(r+1)*BLK,j*BLK:(j+1)*BLK],0)
        for c in range(4):
            for j in range(HEADS): tile(1,0,c,j,self.out.at[j*BLK:(j+1)*BLK,c*BLK:(c+1)*BLK],2)
        for r in range(4):
            for c in range(2):
                for j in range(HEADS): tile(2,r,c,j,self.up.at[r*BLK:(r+1)*BLK,j*fs+c*BLK:j*fs+(c+1)*BLK],3)
        for r in range(2):
            for c in range(4):
                for j in range(HEADS): tile(3,r,c,j,self.down.at[j*fs+r*BLK:j*fs+(r+1)*BLK,c*BLK:(c+1)*BLK],4)
    def wait(self,*which):
        refs=(self.q,self.kv,self.out,self.up,self.down)
        for k in which: pltpu.make_async_copy(refs[k],refs[k],self.sems.at[k]).wait()

def rows_at(i,n): return pl.ds(pl.multiple_of(i*n,n),n)

CH=160
KB=320

def forward(w,gains,mp,h_full,own_rows,key_hoods,row_hoods,K,V,q,heads,lse,bias,hidden,r1,r2,emit):
    share=q.shape[0]; keys=K.shape[1]; chunks=share//CH
    start=mp*share
    def mask(i,_):
        rows=rows_at(i,CH)
        bias[rows,:]=jnp.where(row_hoods[rows,:]==key_hoods[...],0.0,MASK_VALUE)
        return 0
    lax.fori_loop(0,chunks,mask,0)
    w.wait(1)
    def project(i,_):
        j,kb=i//(keys//KB),i%(keys//KB)
        rows=rows_at(kb,KB)
        kv=nn(h_full[rows,:],w.kv[j]).astype(bf16)
        K[j,rows,:]=kv[:,:HD]; V[j,rows,:]=kv[:,HD:]
        return 0
    lax.fori_loop(0,HEADS*(keys//KB),project,0)
    w.wait(0)
    def queries(i,_):
        rows=rows_at(i,CH)
        x=h_full[pl.ds(pl.multiple_of(start+i*CH,CH),CH),:]
        q[rows,:]=nn(x,w.q[...]).astype(bf16)
        return 0
    lax.fori_loop(0,chunks,queries,0)
    lane=lax.broadcasted_iota(jnp.int32,(CH,BLK),1)
    def attend(i,_):
        rows=rows_at(i,CH)
        stats=jnp.zeros((CH,BLK),f32)
        for j in range(HEADS):
            s=nt(q[rows,j*HD:(j+1)*HD],K[j])+bias[rows,:]
            peak=jnp.max(s,axis=1,keepdims=True)
            p=jnp.exp2((s-peak)*(SCALE*LOG2E))
            total=jnp.sum(p,axis=1,keepdims=True)
            o=nn(p.astype(bf16),V[j])/total
            heads[rows,j*HD:(j+1)*HD]=o.astype(bf16)
            stats=jnp.where(lane==j,peak*(SCALE*LOG2E)+jnp.log2(total),stats)
        lse[rows,:]=stats
        return 0
    lax.fori_loop(0,chunks,attend,0)
    w.wait(2,3,4)
    def rest(i,_):
        rows=rows_at(i,CH)
        a=own_rows(i)+nn(heads[rows,:],w.out[...])
        r1[rows,:]=a
        first=normed(a)[0]*gains[0:1,:]+gains[1:2,:]
        hid=nn(first.astype(bf16),w.up[...])
        hidden[rows,:]=hid
        b=first+nn(gelu(hid).astype(bf16),w.down[...])
        r2[rows,:]=b
        emit(i,normed(b)[0]*gains[2:3,:]+gains[3:4,:])
        return 0
    lax.fori_loop(0,chunks,rest,0)

def backward(w,gains,mp,h_full,upper,key_hoods_col,row_hoods_row,K,V,q,heads,lse,biasT,hidden,r1,r2,
        dm,act,dhid,first,datt,dheads,delta,fg,dq,dkv,dhp,own_part,vec,put):
    share=q.shape[0]; keys=K.shape[1]; chunks=share//CH
    start=mp*share
    lane=lax.broadcasted_iota(jnp.int32,(CH,BLK),1)
    def colsum(v): return jnp.sum(v,axis=0,keepdims=True)
    def mask(i,_):
        rows=rows_at(i,KB)
        biasT[rows,:]=jnp.where(key_hoods_col[rows,:]==row_hoods_row[...],0.0,MASK_VALUE)
        return 0
    lax.fori_loop(0,keys//KB,mask,0)
    w.wait(0,1,2,3,4)
    def part(i,carry):
        rows=rows_at(i,CH)
        dy=upper(i)
        xhat,rho=normed(r2[rows,:])
        g2,s2=colsum(dy*xhat),colsum(dy)
        sg=norm_back(dy,xhat,rho,gains[2:3,:])
        dmb=sg.astype(bf16); dm[rows,:]=dmb
        a,slope=gelu_both(hidden[rows,:])
        act[rows,:]=a.astype(bf16)
        dh=(nt(dmb,w.down[...])*slope).astype(bf16)
        dhid[rows,:]=dh
        fu=sg+nt(dh,w.up[...])
        xhat,rho=normed(r1[rows,:])
        first[rows,:]=(xhat*gains[0:1,:]+gains[1:2,:]).astype(bf16)
        g1,s1=colsum(fu*xhat),colsum(fu)
        f=norm_back(fu,xhat,rho,gains[0:1,:])
        fg[rows,:]=f
        fb=f.astype(bf16); datt[rows,:]=fb
        dhe=nt(fb,w.out[...]).astype(bf16)
        dheads[rows,:]=dhe
        prod=dhe.astype(f32)*heads[rows,:].astype(f32)
        stats=jnp.zeros((CH,BLK),f32)
        for j in range(HEADS):
            stats=jnp.where(lane==j,jnp.sum(prod[:,j*HD:(j+1)*HD],axis=1,keepdims=True),stats)
        delta[rows,:]=stats
        return tuple(c+v for c,v in zip(carry,(g1,s1,g2,s2)))
    zero=jnp.zeros((1,D),f32)
    g1,s1,g2,s2=lax.fori_loop(0,chunks,part,(zero,)*4)
    vec[0:1,:]=g1; vec[1:2,:]=s1; vec[2:3,:]=g2; vec[3:4,:]=s2
    fs=FF//HEADS
    def tiles(kind,j,value,rr=None,c0=0):
        for r in range(value.shape[0]//BLK):
            for c in range(value.shape[1]//BLK):
                put(FIRST_BLOCK[kind]+r*COLS_TILE[kind]+c+c0,j,value[r*BLK:(r+1)*BLK,c*BLK:(c+1)*BLK].astype(bf16))
    for j in range(HEADS):
        tiles(3,j,tn(act[:,j*fs:(j+1)*fs],dm[...]))
        tiles(2,j,tn(first[...],dhid[:,j*fs:(j+1)*fs]))
        tiles(1,j,tn(heads[:,j*HD:(j+1)*HD],datt[...]))
    lseT=jnp.transpose(lse[...]); deltaT=jnp.transpose(delta[...])
    for j in range(HEADS):
        L=lseT[j:j+1,:]; dl=deltaT[j:j+1,:]
        qj=q[:,j*HD:(j+1)*HD]; doj=dheads[:,j*HD:(j+1)*HD]
        def keyblock(kb,acc):
            rows=rows_at(kb,KB)
            k=K[j,rows,:]; v=V[j,rows,:]
            p=jnp.exp2((nt(k,qj)+biasT[rows,:])*(SCALE*LOG2E)-L)
            dv=nn(p.astype(bf16),doj)
            ds=(p*(nt(v,doj)-dl)).astype(bf16)
            dk=nn(ds,qj)*SCALE
            dkv[j,rows,:]=jnp.concatenate([dk,dv],axis=1).astype(bf16)
            return acc+tn(ds,k)
        acc=lax.fori_loop(0,keys//KB,keyblock,jnp.zeros((share,HD),f32))
        dq[:,j*HD:(j+1)*HD]=(acc*SCALE).astype(bf16)
    def own(i,_):
        rows=rows_at(i,CH)
        own_part[rows,:]=fg[rows,:]+nt(dq[rows,:],w.q[...])
        return 0
    lax.fori_loop(0,chunks,own,0)
    def context(kb,_):
        rows=rows_at(kb,KB)
        t=nt(dkv[0,rows,:],w.kv[0])
        for j in range(1,HEADS): t=t+nt(dkv[j,rows,:],w.kv[j])
        dhp[rows,:]=t.astype(bf16)
        return 0
    lax.fori_loop(0,keys//KB,context,0)
    dhp[keys:,:]=jnp.zeros((dhp.shape[0]-keys,D),bf16)
    hown=h_full[pl.ds(pl.multiple_of(start,CH),share),:]
    hctx=h_full[:keys,:]
    for j in range(HEADS):
        tiles(0,j,tn(hown,dq[:,j*HD:(j+1)*HD]))
        tiles(0,j,tn(hctx,dkv[j]),c0=1)
BLK=128; STEP=10
BETA_ONE=0.9; BETA_TWO=0.95; BETA_STATS=0.95; RATE_MATRIX=0.12; DECAY_WEIGHT=0.01; ADAM_EPSILON=1e-8

def split(x):
    hi=x.astype(jnp.bfloat16)
    return hi,(x-hi.astype(jnp.float32)).astype(jnp.bfloat16)
def dot3(a,b,ca,cb):
    dims=(((ca,),(cb,)),((),()))
    ah,al=a; bh,bl=b
    d=lambda x,y: lax.dot_general(x,y,dims,preferred_element_type=jnp.float32)
    return d(ah,bh)+(d(ah,bl)+d(al,bh))
def dotf(a,b,ca,cb):
    return lax.dot_general(a,b,(((ca,),(cb,)),((),())),preferred_element_type=jnp.float32,precision=lax.Precision.HIGHEST)

def soap_kernel(slots, g_ref,m_ref,v_ref,l_ref,r_ref,ql_ref,qr_ref,w_ref, mo,vo,lo,ro,qlo,qro,wo, x_ref, a_ref):
    def first(i,_):
        g=g_ref[i]; ql=split(ql_ref[i]); qr=split(qr_ref[i])
        gs=split(g)
        m=BETA_ONE*m_ref[i]+(1-BETA_ONE)*g
        mo[i]=m
        def turn(v):
            return dot3(split(dot3(ql,v,0,0)),qr,1,0)
        tg=turn(gs)
        v=BETA_TWO*v_ref[i]+(1-BETA_TWO)*tg*tg
        vo[i]=v
        d=turn(split(m))/(1-BETA_ONE**STEP)/(jnp.sqrt(v/(1-BETA_TWO**STEP))+ADAM_EPSILON)
        u=dot3(split(dot3(ql,split(d),1,0)),qr,1,1)
        w=w_ref[i]
        wo[i]=w-RATE_MATRIX*(u+DECAY_WEIGHT*w)
        ln=BETA_STATS*l_ref[i]+(1-BETA_STATS)*dot3(gs,gs,1,1)
        rn=BETA_STATS*r_ref[i]+(1-BETA_STATS)*dot3(gs,gs,0,0)
        lo[i]=ln; ro[i]=rn
        al=dotf(ln,ql_ref[i],1,0); ar=dotf(rn,qr_ref[i],1,0)
        a_ref[2*i]=al; a_ref[2*i+1]=ar
        x_ref[2*i]=dotf(al,al,0,0); x_ref[2*i+1]=dotf(ar,ar,0,0)
        return 0
    lax.fori_loop(0,slots,first,0)
    n=2*slots
    lane=lax.broadcasted_iota(jnp.int32,(8,BLK),1)
    sub=lax.broadcasted_iota(jnp.int32,(8,BLK),0)
    for p in range(BLK//8):
        def step(kk,_):
            k=p*8+kk
            idx=jnp.full((8,BLK),k,jnp.int32)
            atk=lane==k
            below=sub>kk
            rows=[jnp.broadcast_to(x_ref[m,pl.ds(k,1),:],(8,BLK)) for m in range(n)]
            rinv=[1.0/jnp.take_along_axis(row,idx,axis=1) for row in rows]
            scaled=[jnp.where(atk,1.0,row)*ri for row,ri in zip(rows,rinv)]
            for m in range(n):
                for t in range(p,BLK//8):
                    v=x_ref[m,t*8:(t+1)*8,:]
                    f=jnp.take_along_axis(v,idx,axis=1)
                    new=jnp.where(atk,0.0,v)-f*scaled[m]
                    if t==p: new=jnp.where(below,new,v)
                    x_ref[m,t*8:(t+1)*8,:]=new
            return 0
        lax.fori_loop(0,8,step,0)
    r=lax.broadcasted_iota(jnp.int32,(BLK,BLK),0); c=lax.broadcasted_iota(jnp.int32,(BLK,BLK),1)
    def last(i,_):
        for s,out in ((0,qlo),(1,qro)):
            x=x_ref[2*i+s]
            piv=jnp.sum(jnp.where(r==c,x,0.0),axis=1,keepdims=True)
            inv=jnp.where(r==c,1.0,jnp.where(r>c,x,0.0))*lax.rsqrt(piv)
            out[i]=dotf(a_ref[2*i+s],inv,1,1)
        return 0
    lax.fori_loop(0,slots,last,0)

def soap(g,m,v,l,r,ql,qr,w):
    slots=g.shape[0]
    sh=jax.ShapeDtypeStruct((slots,BLK,BLK),jnp.float32)
    vm=pl.BlockSpec(memory_space=pltpu.VMEM)
    return pl.pallas_call(partial(soap_kernel,slots),out_shape=[sh]*7,in_specs=[vm]*8,out_specs=[vm]*7,
        scratch_shapes=[pltpu.VMEM((2*slots,BLK,BLK),jnp.float32)]*2,
        compiler_params=pltpu.CompilerParams(vmem_limit_bytes=48<<20),name="soap")(g,m,v,l,r,ql,qr,w)
def adam_vector(grad, first, second, weight):
    first_new = BETA_ONE * first + (1.0 - BETA_ONE) * grad
    second_new = BETA_TWO * second + (1.0 - BETA_TWO) * grad * grad
    weight_new = weight - RATE_VECTOR * (first_new / (1.0 - BETA_ONE**STEP)) / (
        jnp.sqrt(second_new / (1.0 - BETA_TWO**STEP)) + ADAM_EPSILON
    )
    return (first_new, second_new, weight_new)


def pl_shape(shape,dtype): return jax.ShapeDtypeStruct(shape,dtype)

def first_kernel(slots,owners,h_full,wall,gains,key_hoods,row_hoods,out,out_low,K,V,q,heads,lse,hidden,r1,r2,bias,sems,*wrefs):
    w=Weights(0,owners,wall,slots,wrefs,sems)
    mp=lax.axis_index("mp"); share=q.shape[0]
    def own(i): return h_full[pl.ds(pl.multiple_of(mp*share+i*CH,CH),CH),:].astype(f32)
    def emit(i,v):
        out[rows_at(i,CH),:]=v; out_low[rows_at(i,CH),:]=v.astype(bf16)
    forward(w,gains,mp,h_full,own,key_hoods,row_hoods,K,V,q,heads,lse,bias,hidden,r1,r2,emit)

def second_kernel(slots,owners,h_full,h_own,wall,gains,key_hoods,row_hoods,key_col,row_line,cot,
        layer_out,g2,dhp,own_part,vec,K,V,q,heads,lse,hidden,r1,r2,bias,biasT,dm,act,dhid,first,datt,dheads,delta,fg,dq,dkv,sems,*wrefs):
    w=Weights(1,owners,wall,slots,wrefs,sems)
    mp=lax.axis_index("mp"); share=q.shape[0]
    def emit(i,v): layer_out[rows_at(i,CH),:]=v
    forward(w,gains,mp,h_full,lambda i: h_own[rows_at(i,CH),:],key_hoods,row_hoods,K,V,q,heads,lse,bias,hidden,r1,r2,emit)
    w.wait=lambda *k: None
    def upper(i): return cot[pl.ds(pl.multiple_of(mp*share+i*CH,CH),CH),:].astype(f32)
    def put(b,j,v): g2[b,j]=v
    backward(w,gains,mp,h_full,upper,key_col,row_line,K,V,q,heads,lse,biasT,hidden,r1,r2,dm,act,dhid,first,datt,dheads,delta,fg,dq,dkv,dhp,own_part,vec,put)

def third_kernel(slots,owners,h_full,wall,gains,key_col,row_line,K,V,q,heads,lse,hidden,r1,r2,up,g2,
        gout,dhp,own_part,vec,biasT,dm,act,dhid,first,datt,dheads,delta,fg,dq,dkv,sems,*wrefs):
    w=Weights(0,owners,wall,slots,wrefs,sems)
    mp=lax.axis_index("mp"); share=q.shape[0]
    def place(b):
        slot=owners[b]
        return slot//slots,pl.ds(pl.multiple_of(slot%slots*BLK,BLK),BLK)
    def move(b,_):
        d,rows=place(b+LAYER_BLOCKS)
        for j in range(HEADS): gout[d,j,rows,:]=g2[b,j]
        return 0
    lax.fori_loop(0,LAYER_BLOCKS,move,0)
    def put(b,j,v):
        d,rows=place(b)
        gout[d,j,rows,:]=v
    backward(w,gains,mp,h_full,lambda i: up[rows_at(i,CH),:],key_col,row_line,K,V,q,heads,lse,biasT,hidden,r1,r2,dm,act,dhid,first,datt,dheads,delta,fg,dq,dkv,dhp,own_part,vec,put)

def kept_shapes(share,keys):
    return [((HEADS,keys,HD),bf16),((HEADS,keys,HD),bf16),((share,D),bf16),((share,D),bf16),((share,BLK),f32),((share,FF),f32),((share,D),f32),((share,D),f32)]
def back_scratch(share,keys):
    v=pltpu.VMEM
    return [v((keys,share),f32),v((share,D),bf16),v((share,FF),bf16),v((share,FF),bf16),v((share,D),bf16),v((share,D),bf16),v((share,D),bf16),
        v((share,BLK),f32),v((share,D),f32),v((share,D),bf16),v((HEADS,keys,2*HD),bf16)]

def params(mib): return pltpu.CompilerParams(vmem_limit_bytes=mib<<20)

def local(tokens,cotangent,context_sizes,query_hoods,owners,master_blocks,first_blocks,second_blocks,left_blocks,right_blocks,
        left_bases,right_bases,vector_master,vector_moment,vector_square):
    dp=lax.axis_size("dp"); mp=lax.axis_index("mp")
    rows=tokens.shape[0]; keys=rows-query_hoods.shape[0]; share=rows//HEADS; slots=master_blocks.shape[0]
    n=vector_master.shape[0]
    high=vector_master.astype(bf16)
    rest=(vector_master-high.astype(f32)).astype(bf16)
    extra=jnp.pad(jnp.stack([high,rest]),((0,14),(0,BLK-n)))
    slab=jnp.concatenate([master_blocks.astype(bf16).reshape(slots*BLK,BLK),extra],axis=0)
    wall=gather_all(slab,dp,0)
    pair=wall[:,:,slots*BLK:slots*BLK+2,:n].astype(f32)
    gains=(pair[:,:,0]+pair[:,:,1]).reshape(LAYERS,4,D)
    sizes=context_sizes[0]
    order=jnp.arange(sizes.shape[0],dtype=jnp.int32)
    ends=jnp.sum(jnp.where(order[None,:]<=order[:,None],sizes[None,:],0),axis=1)
    positions=jnp.arange(keys,dtype=jnp.int32)
    key_hoods=jnp.sum((positions[:,None]>=ends[None,:]).astype(jnp.int32),axis=1)
    own_hoods=lax.dynamic_slice_in_dim(jnp.concatenate([key_hoods,query_hoods]),mp*share,share)
    key_line,key_col=key_hoods[None,:],key_hoods[:,None]
    row_line,row_col=own_hoods[None,:],own_hoods[:,None]
    kept=kept_shapes(share,keys)
    wsc=[pltpu.SemaphoreType.DMA((5,))]+weight_shapes()
    V_=VMEM_SPEC
    out=pl.pallas_call(partial(first_kernel,slots),
        out_shape=[pl_shape((share,D),f32),pl_shape((share,D),bf16)]+[pl_shape(*k) for k in kept],
        in_specs=[SMEM_SPEC,V_,ANY_SPEC,V_,V_,V_],out_specs=[V_]*10,
        scratch_shapes=[pltpu.VMEM((share,keys),f32)]+wsc,compiler_params=params(56),name="first_layer")(
        owners,tokens,wall,gains[0],key_line,row_col)
    h_own,h_low,saved=out[0],out[1],out[2:]
    h_full=share_rows(h_low,2)
    layer_out,g2,dhp,own_part,vec2=pl.pallas_call(partial(second_kernel,slots),
        out_shape=[pl_shape((share,D),f32),pl_shape((LAYER_BLOCKS,HEADS,BLK,BLK),bf16),pl_shape((rows,D),bf16),pl_shape((share,D),f32),pl_shape((4,D),f32)],
        in_specs=[SMEM_SPEC,V_,V_,ANY_SPEC]+[V_]*6,out_specs=[V_]*5,
        scratch_shapes=[pltpu.VMEM(*k) for k in kept]+[pltpu.VMEM((share,keys),f32)]+back_scratch(share,keys)+wsc,
        compiler_params=params(60),name="second_layer")(
        owners,h_full,h_own,wall,gains[1],key_line,row_col,key_col,row_line,cotangent)
    upper=total_rows(dhp,own_part,3)
    gout,dhp,own_part,vec1=pl.pallas_call(partial(third_kernel,slots),
        out_shape=[pl_shape(wall.shape,bf16),pl_shape((rows,D),bf16),pl_shape((share,D),f32),pl_shape((4,D),f32)],
        in_specs=[SMEM_SPEC,V_,ANY_SPEC]+[V_]*13,out_specs=[V_]*4,
        scratch_shapes=back_scratch(share,keys)+wsc,
        compiler_params=params(60),name="first_layer_back")(
        owners,tokens,wall,gains[0],key_col,row_line,*saved,upper,g2)
    tokens_grad=total_rows(dhp,own_part,4)
    vec=jnp.stack([vec1,vec2]).astype(bf16).reshape(dp,HEADS,1,n)
    vec=jnp.pad(vec,((0,0),(0,0),(0,15),(0,BLK-n)))
    gout=lax.dynamic_update_slice(gout,vec,(0,0,slots*BLK,0))
    total=reduce_all(gout,1)
    results=soap(total[:slots*BLK].reshape(slots,BLK,BLK),first_blocks,second_blocks,left_blocks,right_blocks,left_bases,right_bases,master_blocks)
    vector_results=adam_vector(total[slots*BLK,:n],vector_moment,vector_square,vector_master)
    return (layer_out,tokens_grad)+tuple(results)+vector_results


def solution(mesh):
    return jax.shard_map(
        local,
        mesh=mesh,
        in_specs=(
            P("dp", None),
            P("dp", None),
            P("dp", None),
            P("dp"),
            P(),
            P("dp", "mp", None),
            P("dp", "mp", None),
            P("dp", "mp", None),
            P("dp", "mp", None),
            P("dp", "mp", None),
            P("dp", "mp", None),
            P("dp", "mp", None),
            P(("dp", "mp")),
            P(("dp", "mp")),
            P(("dp", "mp")),
        ),
        out_specs=(
            P(("dp", "mp"), None),
            P(("dp", "mp"), None),
            P("dp", "mp", None),
            P("dp", "mp", None),
            P("dp", "mp", None),
            P("dp", "mp", None),
            P("dp", "mp", None),
            P("dp", "mp", None),
            P("dp", "mp", None),
            P(("dp", "mp")),
            P(("dp", "mp")),
            P(("dp", "mp")),
        ),
        check_vma=False,
    )
```

time: 745 us -> 321 us (0.43); the launches traced: 736 us -> 320 us
  waiting for transfers between devices: 359 us -> 0 us
  Pallas kernels: 46.1 us -> 298 us
  matrix products: 110 us -> 0 us
  other arithmetic: 71.3 us -> 6.28 us
  local copies, waits for them, and re-layouts: 71 us -> 15.4 us
  blocking collectives: 38.5 us -> 0 us
  starting transfers between devices: 23.2 us -> 0 us
  between operations: 15.4 us -> 0.96 us
    psum x8 -> x0, waiting for transfers between devices: 306 us -> none  [the longest x4 165 us: grad_total(): return lax.psum(partial_sum.astype(jnp.bfloat16), 'mp').astype(jnp.float32)]
    pallas_call x0 -> x8, Pallas kernels: none -> 252 us  [the longest x1 51.5 us: local(): pl.pallas_call(partial(second_kernel, slots), out_shape=[pl_shape((share,...]
    dot_general x68 -> x0, matrix products: 110 us -> none  [the longest x20 41.2 us: inner_rows(): lax.dot_general(left, right, (((0,), (0,)), ((), ())), preferred_element_...]
    all_gather x1 -> x0, waiting for transfers between devices: 52.8 us -> none  [local(): lax.all_gather(master_blocks.astype(jnp.bfloat16), 'dp', axis=0, tiled=True)]
    reduce_sum x20 -> x0, other arithmetic: 44.9 us -> none  [the longest x4 22.2 us: norm_back(): return (lower, jnp.sum(upper * normed, axis=0), jnp.sum(upper, axis=0))]
    all_gather x1 -> x0, blocking collectives: 38.5 us -> none  [local(): lax.all_gather(vector_master, ('dp', 'mp'), axis=0, tiled=True)]
    psum x8 -> x0, starting transfers between devices: 11.6 us -> none  [the longest x4 11.2 us: grad_total(): return lax.psum(partial_sum.astype(jnp.bfloat16), 'mp').astype(jnp.float32)]
    all_to_all x2 -> x0, starting transfers between devices: 11.5 us -> none  [summed_on_arrival(): lax.all_to_all(in_blocks(array, dim, length), axis, 0, 0, tiled=True)]
  transfers between devices with their start and end apart: 11 -> 0, of which waited for: 9 -> 0; matrix products, arithmetic and copies ran while one was open for 12% -> 0% of each run, Pallas kernels for 0% -> 0%
where the time goes in v2:
time: 321 us; the launch traced here: 320 us
  Pallas kernels  298 us (93%)
  local copies, waits for them, and re-layouts  15.4 us (5%)
  other arithmetic  6.28 us (2%)
    pallas_call x1, Pallas kernels, local(): pl.pallas_call(partial(second_kernel, slots), out_shape=[pl_shape((share,...  51.5 us
    pallas_call x1, Pallas kernels, reduce_all(): pl.pallas_call(partial(reduce_kernel, planes, half), out_shape=jax.ShapeD...  48.8 us
    pallas_call x1, Pallas kernels, soap(): pl.pallas_call(partial(soap_kernel, slots), out_shape=[sh] * 7, in_specs=...  45.9 us
    pallas_call x1, Pallas kernels, gather_all(): pl.pallas_call(partial(gather_kernel, planes, half), out_shape=jax.ShapeD...  44.4 us
    pallas_call x1, Pallas kernels, local(): pl.pallas_call(partial(third_kernel, slots), out_shape=[pl_shape(wall.sha...  40.5 us
    pallas_call x2, Pallas kernels, total_rows(): pl.pallas_call(total_kernel, out_shape=jax.ShapeDtypeStruct((rows, cols),...  29.6 us
    pallas_call x1, Pallas kernels, local(): pl.pallas_call(partial(first_kernel, slots), out_shape=[pl_shape((share,...  22.2 us
    pallas_call x1, Pallas kernels, share_rows(): pl.pallas_call(share_kernel, out_shape=jax.ShapeDtypeStruct((4, rows, col...  14.8 us

profile of v2, /device:TPU:0, one launch (start us, length us, event | category | flops | bytes accessed | tf_op | source)
XLA Modules:
  0.0 320.3 jit_solution(15231916093839291882)
XLA Ops:
  2.3 0.8 fusion.3
  3.6 0.8 copy.32.row_hoods
  4.5 1.1 convert_element_type.33
  6.3 1.2 broadcast_in_dim.37.key_col
  7.5 44.4 %gather_all.1.wall = bf16[8,4,1040,128]{3,2,1,0:T(8,128)(2,1)} custom-call(bf16[1040,128]{1,0:T(8,128)(2,1)} %pad_maximum_fusion.slab), custom_call_target="tpu_custom_call" | custom-call | tf_op jit(solution)/shard_map/gather_all/pallas_call | solution.py:117
  51.9 0.9 slice_convert_fusion
  54.1 22.2 %first_layer.1 = (f32[480,512]{1,0:T(8,128)}, bf16[480,512]{1,0:T(8,128)(2,1)}, bf16[4,1600,128]{2,1,0:T(8,128)(2,1)}, bf16[4,1600,128]{2,1,0:T(8,128)(2,1)}, bf...) custom-call(s32[64]{0:T(128)} %owners.5, ...), custom_call_target="tpu_custom_call" | custom-call | tf_op jit(solution)/shard_map/first_layer/pallas_call | solution.py:618
  76.3 1.0 copy-done.13
  77.3 14.8 %share_rows.1 = bf16[4,480,512]{2,1,0:T(8,128)(2,1)S(1)} custom-call(bf16[480,512]{1,0:T(8,128)(2,1)S(1)} %copy-done.13), custom_call_target="tpu_custom_call" | custom-call | tf_op jit(solution)/shard_map/share_rows/pallas_call | solution.py:227
  92.1 1.3 copy-done
  93.4 51.5 %second_layer.1 = (f32[480,512]{1,0:T(8,128)}, bf16[32,4,128,128]{3,2,1,0:T(8,128)(2,1)}, bf16[1920,512]{1,0:T(8,128)(2,1)}, f32[480,512]{1,0:T(8,128)}, f32[4,512]{1,0:T(4,128)}) custom-call(s32[64]{0:T(128)} %owners.5, bf16[1920,512]{1,0:T(8,128)(2,1)} %bitcast.31, f32[480,512]{1,0:T(8,128)} %get-tuple-element.39.h_own, ...), custom_call_target="tpu_custom_call" | custom-call | tf_op jit(solution)/shard_map/second_layer/pallas_call | solution.py:625
  144.9 1.5 copy-done.4
  146.5 1.2 copy-done.6
  147.7 15.1 %total_rows.2.up = f32[480,512]{1,0:T(8,128)S(1)} custom-call(bf16[4,480,512]{2,1,0:T(8,128)(2,1)S(1)} %bitcast.34, f32[480,512]{1,0:T(8,128)S(1)} %copy-done.6), custom_call_target="tpu_custom_call" | custom-call | tf_op jit(solution)/shard_map/total_rows/pallas_call | solution.py:260
  162.7 0.9 copy-done.1
  163.7 40.5 %first_layer_back.1 = (bf16[8,4,1040,128]{3,2,1,0:T(8,128)(2,1)}, bf16[1920,512]{1,0:T(8,128)(2,1)}, f32[480,512]{1,0:T(8,128)}, f32[4,512]{1,0:T(4,128)}) custom-call(s32[64]{0:T(128)} %owners.5, bf16[1920,512]{1,0:T(8,128)(2,1)} %h_full.3, bf16[8,4,1040,128]{3,2,1,0:T(8,128)(2,1)} %gather_all.1.wall, f32[4,512]{1,0:T(4,128)} %bitcast.37, ...), custom_call_target="tpu_custom_call" | custom-call | tf_op jit(solution)/shard_map/first_layer_back/pallas_call | solution.py:632
  204.2 1.5 copy-done.3
  205.7 1.2 copy-done.5
  206.9 14.6 %total_rows.3 = f32[480,512]{1,0:T(8,128)S(1)} custom-call(bf16[4,480,512]{2,1,0:T(8,128)(2,1)S(1)} %bitcast.33, f32[480,512]{1,0:T(8,128)S(1)} %copy-done.5), custom_call_target="tpu_custom_call" | custom-call | tf_op jit(solution)/shard_map/total_rows/pallas_call | solution.py:260
  222.3 48.8 %reduce_all.1 = f32[1040,128]{1,0:T(8,128)} custom-call(bf16[8,4,1040,128]{3,2,1,0:T(8,128)(2,1)} %pad_dynamic-update-slice_fusion.g), custom_call_target="tpu_custom_call" | custom-call | tf_op jit(solution)/shard_map/reduce_all/pallas_call | solution.py:199
  271.1 1.2 divide_subtract_fusion
  272.3 1.1 slice.31
  273.5 45.9 %soap.1 = (f32[8,128,128]{2,1,0:T(8,128)}, f32[8,128,128]{2,1,0:T(8,128)}, f32[8,128,128]{2,1,0:T(8,128)}, f32[8,128,128]{2,1,0:T(8,128)}, f32[8,128,128]{2,1,0:...) custom-call(f32[8,128,128]{2,1,0:T(8,128)S(1)} %bitcast.32, f32[8,128,128]{2,1,0:T(8,128)S(1)} %copy-done.7, ...), custom_call_target="tpu_custom_call" | custom-call | tf_op jit(solution)/shard_map/soap/pallas_call | solution.py:536
  319.4 0.9 copy.45
  (47 shorter events, 5.0 us)
Async XLA Ops:
  3.0 48.9 %copy-start.14 = (s32[480]{0:T(512)}, s32[480]{0:T(512)S(1)}, u32[]{:S(2)}) copy-start(s32[480]{0:T(512)S(1)} %fusion.3) | copy-start | bytes 5764
  76.3 1.0 copy-start.13
  92.1 1.3 copy-start
  144.9 1.5 copy-start.4
  146.5 1.2 copy-start.6
  162.7 0.9 copy-start.1
  204.2 1.5 copy-start.3
  205.7 1.2 copy-start.5
  206.9 14.6 %copy-start.15 = (f32[4,512]{1,0:T(4,128)S(1)}, f32[4,512]{1,0:T(4,128)}, u32[]{:S(2)}) copy-start(f32[4,512]{1,0:T(4,128)} %get-tuple-element.56) | copy-start | bytes 24580
  206.9 14.6 %copy-start.16 = (f32[4,512]{1,0:T(4,128)S(1)}, f32[4,512]{1,0:T(4,128)}, u32[]{:S(2)}) copy-start(f32[4,512]{1,0:T(4,128)} %get-tuple-element.55) | copy-start | bytes 24580
  222.2 48.9 %copy-start.17 = (f32[128]{0:T(128)S(1)}, f32[128]{0:T(128)}, u32[]{:S(2)}) copy-start(f32[128]{0:T(128)} %param.27) | copy-start | bytes 1540
  222.2 48.9 %copy-start.18 = (f32[128]{0:T(128)S(1)}, f32[128]{0:T(128)}, u32[]{:S(2)}) copy-start(f32[128]{0:T(128)} %param.29) | copy-start | bytes 1540
  222.2 48.9 %copy-start.19 = (f32[128]{0:T(128)S(1)}, f32[128]{0:T(128)}, u32[]{:S(2)}) copy-start(f32[128]{0:T(128)} %param.28) | copy-start | bytes 1540
  222.2 51.2 %copy-start.2 = (f32[8,128,128]{2,1,0:T(8,128)S(1)}, f32[8,128,128]{2,1,0:T(8,128)}, u32[]{:S(2)}) copy-start(f32[8,128,128]{2,1,0:T(8,128)} %w_ref.1) | copy-start | bytes 1572868
  222.2 51.2 %copy-start.7 = (f32[8,128,128]{2,1,0:T(8,128)S(1)}, f32[8,128,128]{2,1,0:T(8,128)}, u32[]{:S(2)}) copy-start(f32[8,128,128]{2,1,0:T(8,128)} %m_ref.1) | copy-start | bytes 1572868
  222.3 51.2 %copy-start.8 = (f32[8,128,128]{2,1,0:T(8,128)S(1)}, f32[8,128,128]{2,1,0:T(8,128)}, u32[]{:S(2)}) copy-start(f32[8,128,128]{2,1,0:T(8,128)} %v_ref.1) | copy-start | bytes 1572868
  222.3 51.2 %copy-start.9 = (f32[8,128,128]{2,1,0:T(8,128)S(1)}, f32[8,128,128]{2,1,0:T(8,128)}, u32[]{:S(2)}) copy-start(f32[8,128,128]{2,1,0:T(8,128)} %l_ref.1) | copy-start | bytes 1572868
  222.3 51.2 %copy-start.10 = (f32[8,128,128]{2,1,0:T(8,128)S(1)}, f32[8,128,128]{2,1,0:T(8,128)}, u32[]{:S(2)}) copy-start(f32[8,128,128]{2,1,0:T(8,128)} %r_ref.1) | copy-start | bytes 1572868
  222.3 51.2 %copy-start.11 = (f32[8,128,128]{2,1,0:T(8,128)S(1)}, f32[8,128,128]{2,1,0:T(8,128)}, u32[]{:S(2)}) copy-start(f32[8,128,128]{2,1,0:T(8,128)} %ql_ref.1) | copy-start | bytes 1572868
  222.3 51.2 %copy-start.12 = (f32[8,128,128]{2,1,0:T(8,128)S(1)}, f32[8,128,128]{2,1,0:T(8,128)}, u32[]{:S(2)}) copy-start(f32[8,128,128]{2,1,0:T(8,128)} %qr_ref.1) | copy-start | bytes 1572868
